TPU v7x, 32 devices: a whole 2x2x4 slice. The times are simulated.
32 devices in a mesh: node: 4 (over y, x), dev: 8 (over z, core).
Axes of the slice: x: 2, y: 2, z: 4, core: 2. Of those that a mesh axis runs over, the one named last changes fastest.
Arguments:
- state: float32 [72, 8, 8192], P(None, None, ('node', 'dev')), may hold values from -6 to 6
- span_owner: int32 [8192, 1], P(('node', 'dev')), may hold values from 0 to 31; in each aligned block of 256 rows (0 to 255, 256 to 511, ...) at most 16 rows name the same one
- regime: int32 [8192], P(('node', 'dev')), may hold values from 0 to 2
- moments: float32 [72, 8, 16384], P(None, None, ('node', 'dev')), may hold values from -6 to 6
- remap_weights: float32 [128, 128, 128], P(('node', 'dev')), may hold values from -0.5 to 0.5
- remap_rows: int32 [128], P(('node', 'dev')), may hold values from 0 to 127
- remap_cols: int32 [128], P(('node', 'dev')), may hold values from 0 to 1
Outputs:
- tendencies: float32 [72, 8, 8192], P(None, None, ('node', 'dev'))
- moments_out: float32 [72, 8, 16384], P(None, None, ('node', 'dev'))
- ocean_flux: float32 [128, 4, 128], P(('node', 'dev'))
Inputs may be any that keep to these rules, and one draw needn't show every extreme that they name: `span_owner`: among the 256 columns of one device no owner is named more than 16 times; some device names some owner exactly 16 times.
All inputs are finite; a program needn't handle non-finite values.
Results may differ from a plain program's by a relative error of at most 0.00014.
Values sent between devices are 32-bit elements; how exact they have to be, the bound alone decides.
A program may use at most 64 MiB of HBM per device.

v0:
```python
import jax
import jax.numpy as jnp
from jax import lax
from jax.sharding import PartitionSpec as P

MICRO_SUB = 2
TURB_ITERS = 3
OBLK_DEV = 4


def level_grad(field):
    padded = jnp.concatenate([field[:1], field, field[-1:]], axis=0)
    return padded[:-2] - padded[2:]


def microphysics(current, column_moments, regime_real):
    temper = current[:, 0]
    vapour = jax.nn.softplus(current[:, 1])
    liquid = jax.nn.softplus(current[:, 2])
    rain_q = jax.nn.softplus(current[:, 3])
    ice_q = jax.nn.softplus(current[:, 4])
    satur = 0.6 * jnp.exp(0.5 * jnp.tanh(0.5 * temper))
    cloudy = 0.5 + jax.nn.sigmoid(column_moments[:, 2] + vapour - satur)
    conden = 0.4 * jnp.tanh(vapour - satur) * cloudy
    autoconv = 0.3 * liquid * liquid / (1.0 + liquid)
    evapor = 0.1 * rain_q * jax.nn.sigmoid(satur - vapour)
    freeze = 0.3 * liquid * jax.nn.sigmoid(-temper)
    melting = 0.2 * ice_q * jax.nn.sigmoid(temper)
    deposit = 0.35 * jnp.tanh(vapour - 0.8 * satur) * cloudy
    aggreg = 0.25 * ice_q * ice_q / (1.0 + ice_q)
    is_warm = (regime_real == 0.0).astype(current.dtype)[None, :]
    is_mixed = (regime_real == 1.0).astype(current.dtype)[None, :]
    is_icy = (regime_real == 2.0).astype(current.dtype)[None, :]
    falling = 0.5 * rain_q
    from_above = jnp.concatenate([jnp.zeros_like(falling[:1]), falling[:-1]], axis=0)
    d_temp = (
        is_warm * (0.8 * (conden - evapor))
        + is_mixed * (0.8 * conden + 0.5 * (freeze - melting))
        + is_icy * (deposit + 0.5 * freeze)
    )
    d_vapour = is_warm * (evapor - conden) - is_mixed * conden - is_icy * deposit
    d_liquid = (
        is_warm * (conden - autoconv) + is_mixed * (conden - freeze - autoconv) - is_icy * freeze
    )
    d_rain = (
        is_warm * (autoconv - evapor)
        + is_mixed * (autoconv + melting)
        + is_icy * aggreg
        + from_above
        - falling
    )
    d_ice = is_mixed * (freeze - melting) + is_icy * (deposit + freeze - aggreg)
    return jnp.stack(
        [
            temper + 0.5 * d_temp,
            current[:, 1] + 0.5 * d_vapour,
            current[:, 2] + 0.5 * d_liquid,
            current[:, 3] + 0.5 * d_rain,
            current[:, 4] + 0.5 * d_ice,
            current[:, 5],
            current[:, 6],
            current[:, 7],
        ],
        axis=1,
    )


def diffusivity(mixed_state, column_moments):
    diff_u = mixed_state[:-1, 5] - mixed_state[1:, 5]
    diff_v = mixed_state[:-1, 6] - mixed_state[1:, 6]
    diff_t = mixed_state[:-1, 0] - mixed_state[1:, 0]
    shear_sq = diff_u * diff_u + diff_v * diff_v
    energy = 0.5 + 60.0 * jax.nn.sigmoid(2.0 * (column_moments[:-1, 0] + column_moments[1:, 0]))
    return (0.3 + 1.5 * shear_sq / (1.0 + shear_sq) * jax.nn.sigmoid(-2.0 * diff_t)) * energy


def implicit(kappa_int, right_side):
    level_count = right_side.shape[0]
    zero_kappa = jnp.zeros_like(kappa_int[0])
    c_prev = zero_kappa
    d_prev = jnp.zeros_like(right_side[0])
    c_rows = []
    d_rows = []
    for level in range(level_count):
        k_low = kappa_int[level - 1] if level > 0 else zero_kappa
        k_high = kappa_int[level] if level < level_count - 1 else zero_kappa
        denominator = 1.0 + k_low + k_high + k_low * c_prev
        c_now = -k_high / denominator
        d_now = (right_side[level] + k_low[None, :] * d_prev) / denominator[None, :]
        c_rows.append(c_now)
        d_rows.append(d_now)
        c_prev = c_now
        d_prev = d_now
    y_next = jnp.zeros_like(right_side[0])
    solved_rows = [None] * level_count
    for level in range(level_count - 1, -1, -1):
        y_now = d_rows[level] - c_rows[level][None, :] * y_next
        solved_rows[level] = y_now
        y_next = y_now
    return jnp.stack(solved_rows, axis=0)


def turbulence(after_micro, column_moments):
    right_side = jnp.concatenate([after_micro[:, 0:2], after_micro[:, 5:8]], axis=1)
    mixed_state = after_micro
    for iteration in range(TURB_ITERS):
        kappa_int = diffusivity(mixed_state, column_moments)
        solved = implicit(kappa_int, right_side)
        mixed_state = jnp.concatenate([solved[:, 0:2], after_micro[:, 2:5], solved[:, 2:5]], axis=1)
    return mixed_state


def gradients_of(mixed_state):
    return jnp.stack(
        [
            level_grad(mixed_state[:, 5]),
            level_grad(mixed_state[:, 6]),
            level_grad(mixed_state[:, 0]),
            level_grad(mixed_state[:, 1]),
        ],
        axis=1,
    )


def moments_from_grads(grads, column_moments):
    grad_u = grads[:, 0]
    grad_v = grads[:, 1]
    grad_t = grads[:, 2]
    grad_q = grads[:, 3]
    production = [
        grad_u * grad_u + grad_v * grad_v,
        grad_t * grad_t,
        grad_q * grad_q,
        grad_t * grad_q,
        grad_u * grad_t,
        grad_v * grad_t,
        grad_u * grad_q,
        grad_u * grad_v,
    ]
    updated = [
        column_moments[:, index]
        + 0.5 * (jnp.tanh(production[index]) - (0.3 + 0.1 * index) * column_moments[:, index])
        for index in range(8)
    ]
    return jnp.stack(updated, axis=1)


def column_physics(columns, column_moments, regime_real):
    after_micro = columns
    for substep in range(MICRO_SUB):
        after_micro = microphysics(after_micro, column_moments, regime_real)
    return turbulence(after_micro, column_moments)


def surface(state, tendencies):
    bottom = state[-1] + tendencies[-1]
    wind_speed = jnp.sqrt(1.0 + bottom[5] * bottom[5] + bottom[6] * bottom[6])
    return jnp.stack(
        [
            -0.5 * wind_speed * bottom[5],
            -0.5 * wind_speed * bottom[6],
            0.5 * jax.nn.softplus(bottom[3]),
            -0.3 * wind_speed * bottom[0],
        ],
        axis=0,
    )


def local(state, span_owner, regime, moments, remap_weights, remap_rows, remap_cols):
    node_count = lax.axis_size("node")
    dev_count = lax.axis_size("dev")
    peer_count = node_count * dev_count
    level_count = state.shape[0]
    col_count = state.shape[2]
    capacity = max(2, 2 * col_count // peer_count)
    slots_total = capacity * peer_count
    owner_ids = span_owner[:, 0]
    one_hot = (owner_ids[:, None] == jnp.arange(peer_count, dtype=jnp.int32)[None, :]).astype(
        jnp.int32
    )
    rank_in = jnp.sum((jnp.cumsum(one_hot, axis=0) - one_hot) * one_hot, axis=1)
    slot_of = rank_in * peer_count + owner_ids
    source = (
        jnp.full((slots_total,), col_count, jnp.int32)
        .at[slot_of]
        .set(jnp.arange(col_count, dtype=jnp.int32))
    )
    regime_real = regime.astype(jnp.float32)
    picked = jnp.stack([moments[:, 0], moments[:, 2]], axis=1).reshape(
        level_count, 2, capacity, peer_count
    )
    fetched = lax.all_to_all(picked, ("node", "dev"), split_axis=3, concat_axis=3, tiled=True)
    part_moments = jnp.take(fetched.reshape(level_count, 2, slots_total), slot_of, axis=2)
    holder = jnp.stack(
        [part_moments[:, 0], jnp.zeros_like(part_moments[:, 0]), part_moments[:, 1]], axis=1
    )
    mixed_state = column_physics(state, holder, regime_real)
    tendencies = mixed_state - state
    grads = gradients_of(mixed_state)
    outgoing = jnp.take(grads, source, axis=2, mode="fill", fill_value=0.0)
    outgoing = outgoing.reshape(level_count, 4, capacity, peer_count)
    live_flags = (source < col_count).astype(jnp.float32).reshape(1, 1, capacity, peer_count)
    back_grads = lax.all_to_all(outgoing, ("node", "dev"), split_axis=3, concat_axis=3, tiled=True)
    back_flags = lax.all_to_all(
        live_flags, ("node", "dev"), split_axis=3, concat_axis=3, tiled=True
    )
    new_moments = moments_from_grads(back_grads.reshape(level_count, 4, slots_total), moments)
    live_slots = (back_flags.reshape(slots_total) > 0.5)[None, None, :]
    moments_out = jnp.where(live_slots, new_moments, moments)
    fluxes = surface(state, tendencies)
    tile_width = remap_weights.shape[1]
    flux_blocks = fluxes.reshape(4, col_count // tile_width, tile_width)[:, remap_cols]
    products = jnp.einsum(
        "fbt,bts->bfs", flux_blocks, remap_weights, precision=lax.Precision.HIGHEST
    )
    targets = jnp.arange(OBLK_DEV * lax.axis_size(("node", "dev")), dtype=jnp.int32)
    selector = (remap_rows[:, None] == targets[None, :]).astype(jnp.float32)
    ocean_flux = lax.psum_scatter(
        jnp.einsum("br,bfs->rfs", selector, products, precision=lax.Precision.HIGHEST),
        ("node", "dev"),
        scatter_dimension=0,
        tiled=True,
    )
    return (tendencies, moments_out, ocean_flux)


def solution(mesh):
    return jax.shard_map(
        local,
        mesh=mesh,
        in_specs=(
            P(None, None, ("node", "dev")),
            P(("node", "dev"), None),
            P(("node", "dev")),
            P(None, None, ("node", "dev")),
            P(("node", "dev"), None, None),
            P(("node", "dev")),
            P(("node", "dev")),
        ),
        out_specs=(
            P(None, None, ("node", "dev")),
            P(None, None, ("node", "dev")),
            P(("node", "dev"), None, None),
        ),
        check_vma=False,
    )
```

profile of v0, /device:TPU:0, one launch (start us, length us, event | category | flops | bytes accessed | tf_op | source)
XLA Modules:
  0.0 436.9 jit_solution(12464591608957055167)
XLA Ops:
  12.4 7.3 %all-to-all-start.1 = ((f32[1,1,16,32]{2,1,0,3:T(1,128)}), f32[1,1,16,32]{2,1,0,3:T(1,128)S(1)}, u32[]{:S(2)}, u32[]{:S(2)}) async-start(f32[1,1,16,32]{2,1,0,3:T(1,128)} %copy.11275), calls=%async_computation.1 | async-start | bytes 32768 | tf_op jit(solution)/shard_map/all_to_all | solution.py:204
  21.7 1.8 copy.10851
  26.9 5.8 %all-to-all-start = ((f32[72,2,16,32]{0,2,1,3:T(8,128)}), f32[72,2,16,32]{0,2,1,3:T(8,128)S(1)}, u32[]{:S(2)}, u32[]{:S(2)}) async-start(f32[72,2,16,32]{0,2,1,3:T(8,128)} %copy.10853), calls=%async_computation | async-start | bytes 1048576 | tf_op jit(solution)/shard_map/all_to_all | solution.py:192
  33.6 1.6 divide_multiply_fusion.2
  35.9 13.2 %all-to-all-done = f32[72,2,16,32]{0,2,1,3:T(8,128)S(1)} async-done(((f32[72,2,16,32]{0,2,1,3:T(8,128)}), f32[72,2,16,32]{0,2,1,3:T(8,128)S(1)}, u32[]{:S(2)}, u32[]{:S(2)}) %all-to-all-start) | async-done | bytes 294944 | tf_op jit(solution)/shard_map/all_to_all | solution.py:192
  49.8 1.7 gather_fusion
  54.4 2.1 fusion.3
  56.4 4.8 %multiply_add_fusion = (f32[72,1,256]{2,1,0:T(1,128)}, f32[72,1,256]{2,1,0:T(1,128)}, f32[72,1,256]{2,1,0:T(1,128)}, f32[72,1,256]{2,1,0:T(1,128)}, f32[72,1,256...) fusion(f32[72,1,256]{2,1,0:T(1,128)S(1)} %get-tuple-element.123, ...), kind=kLoop, calls=%fused_computation.151 | loop fusion | flops 1916928 | bytes 1626112 | tf_op jit(solution)/shard_map/add | solution.py:59
  107.9 13.3 %stack.556 = f32[71,5,256]{2,0,1:T(8,128)} concatenate(f32[1,5,256]{2,0,1:T(1,128)} %copy.10894, f32[1,5,256]{2,0,1:T(1,128)} %copy.10895, f32[1,5,256]{2,0,1:T(1,128)} %copy.10896, f32[1,5,256]{2,0,1:T(1,128)} %copy.10897, f32[1,5,256]{2,0,1:T(1,128)} %copy.10898, f32[1,5,256]{2,0,1:T(1,128)} %copy.10899, f32[1,5,256]{2,0,1:T(1,128)} %copy.10900, f32[1,5,256]{2,0,1:T(1,128)} %copy.10901, ...), dimensions={0} | concatenate | bytes 727040 | tf_op jit(solution)/shard_map/stack | solution.py:100
  121.1 1.6 fusion.454
  122.8 13.3 %stack.554 = f32[71,5,256]{2,0,1:T(8,128)} concatenate(f32[1,5,256]{2,0,1:T(1,128)} %copy.10893, f32[1,5,256]{2,0,1:T(1,128)} %copy.10894, f32[1,5,256]{2,0,1:T(1,128)} %copy.10895, f32[1,5,256]{2,0,1:T(1,128)} %copy.10896, f32[1,5,256]{2,0,1:T(1,128)} %copy.10897, f32[1,5,256]{2,0,1:T(1,128)} %copy.10898, f32[1,5,256]{2,0,1:T(1,128)} %copy.10899, f32[1,5,256]{2,0,1:T(1,128)} %copy.10900, ...), dimensions={0} | concatenate | bytes 727040 | tf_op jit(solution)/shard_map/stack | solution.py:100
  183.4 13.3 %stack.596 = f32[71,5,256]{2,0,1:T(8,128)} concatenate(f32[1,5,256]{2,0,1:T(1,128)} %copy.11045, f32[1,5,256]{2,0,1:T(1,128)} %copy.11046, f32[1,5,256]{2,0,1:T(1,128)} %copy.11047, f32[1,5,256]{2,0,1:T(1,128)} %copy.11048, f32[1,5,256]{2,0,1:T(1,128)} %copy.11049, f32[1,5,256]{2,0,1:T(1,128)} %copy.11050, f32[1,5,256]{2,0,1:T(1,128)} %copy.11051, f32[1,5,256]{2,0,1:T(1,128)} %copy.11052, ...), dimensions={0} | concatenate | bytes 727040 | tf_op jit(solution)/shard_map/stack | solution.py:100
  196.7 1.6 fusion.452
  198.3 13.3 %stack.594 = f32[71,5,256]{2,0,1:T(8,128)} concatenate(f32[1,5,256]{2,0,1:T(1,128)} %copy.11044, f32[1,5,256]{2,0,1:T(1,128)} %copy.11045, f32[1,5,256]{2,0,1:T(1,128)} %copy.11046, f32[1,5,256]{2,0,1:T(1,128)} %copy.11047, f32[1,5,256]{2,0,1:T(1,128)} %copy.11048, f32[1,5,256]{2,0,1:T(1,128)} %copy.11049, f32[1,5,256]{2,0,1:T(1,128)} %copy.11050, f32[1,5,256]{2,0,1:T(1,128)} %copy.11051, ...), dimensions={0} | concatenate | bytes 727040 | tf_op jit(solution)/shard_map/stack | solution.py:100
  245.0 6.1 %stack.635 = f32[72,5,256]{2,0,1:T(8,128)S(1)} concatenate(f32[1,5,256]{2,0,1:T(1,128)S(1)} %copy.11195, f32[1,5,256]{2,0,1:T(1,128)} %copy.11196, f32[1,5,256]{2,0,1:T(1,128)} %copy.11197, f32[1,5,256]{2,0,1:T(1,128)} %copy.11198, f32[1,5,256]{2,0,1:T(1,128)} %copy.11199, f32[1,5,256]{2,0,1:T(1,128)} %copy.11200, f32[1,5,256]{2,0,1:T(1,128)} %copy.11201, f32[1,5,256]{2,0,1:T(1,128)} %copy.11202, ...), dimensions={0} | concatenate | bytes 737280 | tf_op jit(solution)/shard_map/stack | solution.py:100
  259.0 1.5 copy.11282
  260.4 1.6 copy.11277
  262.1 1.6 fusion.23
  263.7 1.6 copy.11290
  265.3 1.6 copy.11283
  271.4 2.3 pad_maximum_fusion.2
  273.7 3.5 gather_fusion.1
  278.7 1.6 copy.11292
  280.3 3.4 all-to-all-start.2
  283.8 1.8 multiply_add_fusion.1
  286.3 2.3 bitcast_dynamic-update-slice_fusion
  288.6 1.5 copy_dynamic-update-slice_fusion
  295.2 2.1 copy.11306
  297.3 124.7 %all-reduce.5.cloned.1.call-done = f32[128,4,128]{2,0,1:T(8,128)} async-done(((f32[128,4,128]{2,0,1:T(8,128)}), f32[128,4,128]{2,0,1:T(8,128)}) %all-reduce.5.cloned.1.call-update) | async-done | bytes 262160
  423.3 1.8 copy.11293
  425.7 1.7 broadcast_select_fusion
  427.3 2.8 copy.11307
  (433 shorter events, 163.6 us)
Async XLA Ops:
  7.2 286.5 %copy-start = (f32[4,128,128]{2,1,0:T(8,128)S(1)}, f32[4,128,128]{2,1,0:T(8,128)}, u32[]{:S(2)}) copy-start(f32[4,128,128]{2,1,0:T(8,128)} %param.11) | copy-start | bytes 786436
  12.4 14.5 %all-to-all-start.1 = ((f32[1,1,16,32]{2,1,0,3:T(1,128)}), f32[1,1,16,32]{2,1,0,3:T(1,128)S(1)}, u32[]{:S(2)}, u32[]{:S(2)}) async-start(f32[1,1,16,32]{2,1,0,3:T(1,128)} %copy.11275), calls=%async_computation.1 | async-start | bytes 32768 | tf_op jit(solution)/shard_map/all_to_all | solution.py:204
  21.1 42.6 %copy-start.17 = (f32[256]{0:T(256)}, f32[256]{0:T(256)S(1)}, u32[]{:S(2)}) copy-start(f32[256]{0:T(256)S(1)} %get-tuple-element.1126) | copy-start | bytes 3076
  21.1 42.6 %copy-start.19 = (f32[256]{0:T(256)}, f32[256]{0:T(256)S(1)}, u32[]{:S(2)}) copy-start(f32[256]{0:T(256)S(1)} %get-tuple-element.1127) | copy-start | bytes 3076
  21.1 42.7 %copy-start.21 = (f32[256]{0:T(256)}, f32[256]{0:T(256)S(1)}, u32[]{:S(2)}) copy-start(f32[256]{0:T(256)S(1)} %get-tuple-element.1128) | copy-start | bytes 3076
  21.7 2.6 copy-start.1
  26.9 22.2 %all-to-all-start = ((f32[72,2,16,32]{0,2,1,3:T(8,128)}), f32[72,2,16,32]{0,2,1,3:T(8,128)S(1)}, u32[]{:S(2)}, u32[]{:S(2)}) async-start(f32[72,2,16,32]{0,2,1,3:T(8,128)} %copy.10853), calls=%async_computation | async-start | bytes 1048576 | tf_op jit(solution)/shard_map/all_to_all | solution.py:192
  53.0 10.0 %copy-start.3 = (f32[71,256]{1,0:T(8,128)}, f32[71,256]{1,0:T(8,128)S(1)}, u32[]{:S(2)}) copy-start(f32[71,256]{1,0:T(8,128)S(1)} %copy.10892) | copy-start | bytes 218116
  54.3 9.4 %copy-start.12 = (f32[72,1,256]{2,1,0:T(1,128)}, f32[72,1,256]{2,1,0:T(1,128)S(1)}, u32[]{:S(2)}) copy-start(f32[72,1,256]{2,1,0:T(1,128)S(1)} %get-tuple-element.896) | copy-start | bytes 221188
  54.4 8.7 %copy-start.13 = (f32[71,1,256]{2,1,0:T(1,128)S(1)}, f32[71,1,256]{2,1,0:T(1,128)}, u32[]{:S(2)}) copy-start(f32[71,1,256]{2,1,0:T(1,128)} %add_divide_fusion) | copy-start | bytes 218116
  56.4 7.3 %copy-start.5 = (f32[72,1,256]{2,1,0:T(1,128)}, f32[72,1,256]{2,1,0:T(1,128)S(1)}, u32[]{:S(2)}) copy-start(f32[72,1,256]{2,1,0:T(1,128)S(1)} %get-tuple-element.879) | copy-start | bytes 221188
  56.4 7.6 %copy-start.4 = (f32[72,3,256]{2,1,0:T(4,128)S(1)}, f32[72,3,256]{2,1,0:T(4,128)}, u32[]{:S(2)}) copy-start(f32[72,3,256]{2,1,0:T(4,128)} %slice.1567) | copy-start | bytes 663556
  61.3 2.7 copy-start.7
  61.3 2.7 copy-start.9
  61.3 2.7 copy-start.10
  62.3 1.4 copy-start.11
  63.0 2.4 copy-start.14
  63.0 2.4 copy-start.15
  255.3 18.5 %copy-start.23 = (s32[1024]{0:T(1024)S(1)}, s32[1024]{0:T(1024)}, u32[]{:S(2)}) copy-start(s32[1024]{0:T(1024)} %get-tuple-element.1130) | copy-start | bytes 12292
  271.4 7.1 %copy-start.24 = (pred[16,32]{1,0:T(8,128)(4,1)S(1)}, pred[16,32]{1,0:T(8,128)(4,1)}, u32[]{:S(2)}) copy-start(pred[16,32]{1,0:T(8,128)(4,1)} %broadcast_in_dim.31) | copy-start | bytes 1540
  278.7 5.1 %copy-start.18 = (f32[256]{0:T(256)S(1)}, f32[256]{0:T(256)}, u32[]{:S(2)}) copy-start(f32[256]{0:T(256)} %copy-done.17) | copy-start | bytes 3076
  278.7 5.1 %copy-start.20 = (f32[256]{0:T(256)S(1)}, f32[256]{0:T(256)}, u32[]{:S(2)}) copy-start(f32[256]{0:T(256)} %copy-done.19) | copy-start | bytes 3076
  278.7 5.1 %copy-start.22 = (f32[256]{0:T(256)S(1)}, f32[256]{0:T(256)}, u32[]{:S(2)}) copy-start(f32[256]{0:T(256)} %copy-done.21) | copy-start | bytes 3076
  278.7 7.6 %copy-start.6 = (f32[72,1,256]{2,1,0:T(1,128)S(1)}, f32[72,1,256]{2,1,0:T(1,128)}, u32[]{:S(2)}) copy-start(f32[72,1,256]{2,1,0:T(1,128)} %copy-done.5) | copy-start | bytes 221188
  278.7 7.6 %copy-start.8 = (f32[72,1,256]{2,1,0:T(1,128)S(1)}, f32[72,1,256]{2,1,0:T(1,128)}, u32[]{:S(2)}) copy-start(f32[72,1,256]{2,1,0:T(1,128)} %copy-done.7) | copy-start | bytes 221188
  280.3 142.9 %all-to-all-start.2 = ((f32[72,4,16,32]{0,2,1,3:T(8,128)}), f32[72,4,16,32]{0,2,1,3:T(8,128)}, u32[]{:S(2)}, u32[]{:S(2)}) async-start(f32[72,4,16,32]{0,2,1,3:T(8,128)} %copy.11292), calls=%async_computation.2 | async-start | bytes 2097152 | tf_op jit(solution)/shard_map/all_to_all | solution.py:203
  283.7 8.4 %slice-start = ((f32[72,8,256]{2,1,0:T(8,128)}), f32[1,8,256]{2,1,0:T(8,128)S(1)}, s32[]{:S(2)}) async-start(f32[72,8,256]{2,1,0:T(8,128)} %param.7), calls=%async_computation.4 | async-start | bytes 16384 | tf_op jit(solution)/shard_map/slice | solution.py:156
  283.7 10.3 %copy-start.25 = (s32[4]{0:T(128)S(1)}, s32[4]{0:T(128)}, u32[]{:S(2)}) copy-start(s32[4]{0:T(128)} %param.12) | copy-start | bytes 52
  283.7 138.2 %all-reduce.5.cloned.1.call-start = ((), (), s32[]{:S(2)}) async-start(), calls=%async_computation.3 | async-start | bytes 524288
  286.3 8.8 %copy-start.16 = (f32[1,1,16,32]{3,2,1,0:T(8,128)S(1)}, f32[1,1,16,32]{3,2,1,0:T(8,128)}, u32[]{:S(2)}) copy-start(f32[1,1,16,32]{3,2,1,0:T(8,128)} %copy.11276) | copy-start | bytes 6148
  292.1 0.8 copy-start.2
Sparse Core Ops, SparseCore 0:
  295.2 126.6 all-reduce.4
where the time goes:
time: 440 us; the launch traced here: 437 us
  local copies, waits for them, and re-layouts  220 us (50%)
  waiting for transfers between devices  138 us (31%)
  other arithmetic  45.7 us (10%)
  starting transfers between devices  16.6 us (4%)
  between operations  15.3 us (3%)
    another operation x119, local copies, waits for them, and re-layouts, implicit(): return jnp.stack(solved_rows, axis=0)  126 us
    unnamed x2, waiting for transfers between devices  125 us
    sub x102, local copies, waits for them, and re-layouts, implicit(): y_now = d_rows[level] - c_rows[level][None, :] * y_next  42.5 us
    all_to_all x1, waiting for transfers between devices, local(): lax.all_to_all(picked, ('node', 'dev'), split_axis=3, concat_axis=3, tile...  13.2 us
    unnamed x60, local copies, waits for them, and re-layouts  11.7 us
    slice x8, local copies, waits for them, and re-layouts, level_grad(): padded = jnp.concatenate([field[:1], field, field[-1:]], axis=0)  9.25 us
  transfers between devices with their start and end apart: 4, of which 2 were waited for; matrix products, arithmetic and copies ran while one was open for 6% of the time, Pallas kernels for 0%

commit v1 on v0

v1 whole, which is shorter than its diff:
```python
import functools

import jax
import jax.numpy as jnp
from jax import lax
from jax.experimental import pallas as pl
from jax.experimental.pallas import tpu as pltpu
from jax.sharding import PartitionSpec as P

MICRO_SUB = 2
TURB_ITERS = 3
OBLK_DEV = 4
LANE = 128
SUB = 8
FLUX = 4
GRAD_FIELDS = (5, 6, 0, 1)
F32 = jnp.float32
BF16 = jnp.bfloat16


def plan(peers, cap, levels):
    fetch_rest = 2 * levels - LANE
    back_rest = len(GRAD_FIELDS) * levels - 2 * LANE
    main = max(SUB, cap)
    fetch_rows = max(1, cap * fetch_rest // LANE)
    back_rows = max(1, cap * back_rest // LANE)
    return dict(
        peers=peers,
        cap=cap,
        levels=levels,
        main=main,
        fetch_rest=fetch_rest,
        back_rest=back_rest,
        fetch_rows=fetch_rows,
        back_rows=back_rows,
        fetch_stride=main + SUB,
        back_stride=2 * main + SUB + OBLK_DEV * FLUX,
    )


def sigmoid(x):
    return 0.5 * jnp.tanh(0.5 * x) + 0.5


def softplus(x):
    return jnp.maximum(x, 0.0) + jnp.log(1.0 + jnp.exp(-jnp.abs(x)))


def inverse(x):
    first = pl.reciprocal(x, approx=True)
    return first * (2.0 - x * first)


def split(x):
    high = x.astype(BF16)
    return high, (x - high.astype(F32)).astype(BF16)


def blocks_of(ref, count):
    rows = ref.shape[0] // count
    return [ref.at[pl.ds(block * rows, rows), :] for block in range(count)]


def read_plane(refs, start, rows, stride):
    return jnp.concatenate([ref[pl.ds(start, rows, stride=stride), :] for ref in refs], axis=1)


def write_plane(refs, start, stride, value):
    for block, ref in enumerate(refs):
        ref[pl.ds(start, value.shape[0], stride=stride), :] = value[
            :, block * LANE : (block + 1) * LANE
        ]


def read_tile(refs, cut):
    return jnp.concatenate([ref[cut, :] for ref in refs], axis=1)


def write_tile(refs, cut, value):
    for block, ref in enumerate(refs):
        ref[cut, :] = value[:, block * LANE : (block + 1) * LANE]


def pack_kernel(cfg, *refs):
    levels, peers, cap = cfg["levels"], cfg["peers"], cfg["cap"]
    stride = cfg["fetch_stride"]
    out_ref = refs[-1]
    flat = [ref.reshape(levels * SUB, LANE) for ref in refs[:-1]]
    first = read_plane(flat, 0, levels, SUB)
    third = read_plane(flat, 2, levels, SUB)
    cut = LANE - levels
    main = jnp.concatenate([third, first[:cut]], axis=0).T
    rest = first[cut:]
    for slot in range(cap):
        out_ref[pl.ds(slot, peers, stride=stride), :] = main[slot * peers : (slot + 1) * peers]
    rows = cfg["fetch_rows"]
    groups = cap // rows
    width = rows * peers
    stacked = jnp.concatenate(
        [rest[:, group * width : (group + 1) * width] for group in range(groups)], axis=0
    )
    if stacked.shape[0] < LANE:
        stacked = jnp.concatenate(
            [stacked, jnp.zeros((LANE - stacked.shape[0], width), F32)], axis=0
        )
    if width < LANE:
        stacked = jnp.concatenate([stacked, jnp.zeros((LANE, LANE - width), F32)], axis=1)
    turned = stacked.T
    blank = jnp.zeros((peers, LANE), F32)
    for row in range(cap, cfg["main"]):
        out_ref[pl.ds(row, peers, stride=stride), :] = blank
    for row in range(SUB):
        value = turned[row * peers : (row + 1) * peers] if row < rows else blank
        out_ref[pl.ds(cfg["main"] + row, peers, stride=stride), :] = value


def kappa_tiles(cfg, y_ref, energy_ref, kappa_ref):
    levels = cfg["levels"]
    for tile in range(levels // SUB):
        rows = pl.ds(tile * SUB, SUB)
        here = tile * SUB * SUB

        def drop(field):
            return read_plane(y_ref, here + field, SUB, SUB) - read_plane(
                y_ref, here + SUB + field, SUB, SUB
            )

        diff_u, diff_v, diff_t = drop(5), drop(6), drop(0)
        shear = diff_u * diff_u + diff_v * diff_v
        kappa = (0.3 + 1.5 * shear * inverse(1.0 + shear) * sigmoid(-2.0 * diff_t)) * energy_ref[
            rows, :
        ]
        if tile == levels // SUB - 1:
            level = lax.broadcasted_iota(jnp.int32, kappa.shape, 0)
            kappa = jnp.where(level == SUB - 1, 0.0, kappa)
        kappa_ref[rows, :] = kappa


def solve(cfg, a_ref, kappa_ref, ratio_ref, y_ref):
    levels = cfg["levels"]
    half = levels // 2
    columns = kappa_ref.shape[1]
    zero = jnp.zeros((SUB, columns), F32)

    def tile(level):
        return pl.ds(level * SUB, SUB)

    def kappa_row(level):
        return jnp.broadcast_to(kappa_ref[pl.ds(level, 1), :], (SUB, columns))

    state_of = {0: (zero, zero, zero), 1: (zero, zero, zero)}
    for step in range(half):
        for side in (0, 1):
            level = step if side == 0 else levels - 1 - step
            k_behind, ratio, value = state_of[side]
            k_ahead = kappa_row(level if side == 0 else level - 1)
            scale = inverse((1.0 + k_behind + k_ahead) - k_behind * ratio)
            value = (read_tile(a_ref, tile(level)) + k_behind * value) * scale
            ratio = k_ahead * scale
            write_tile(ratio_ref, tile(level), ratio)
            write_tile(y_ref, tile(level), value)
            state_of[side] = (k_ahead, ratio, value)
    _, ratio_up, value_up = state_of[0]
    _, ratio_low, value_low = state_of[1]
    scale = inverse(1.0 - ratio_up * ratio_low)
    upper = (value_up + ratio_up * value_low) * scale
    lower = (value_low + ratio_low * value_up) * scale
    write_tile(y_ref, tile(half - 1), upper)
    write_tile(y_ref, tile(half), lower)
    for step in range(1, half):
        level = half - 1 - step
        upper = read_tile(y_ref, tile(level)) + read_tile(ratio_ref, tile(level)) * upper
        write_tile(y_ref, tile(level), upper)
        level = half + step
        lower = read_tile(y_ref, tile(level)) + read_tile(ratio_ref, tile(level)) * lower
        write_tile(y_ref, tile(level), lower)


def micro_step(fields, third, above, warm, mixed):
    temper, raw_v, raw_c, raw_r, raw_i = fields
    vapour, liquid, rain_q, ice_q = (softplus(raw) for raw in (raw_v, raw_c, raw_r, raw_i))
    satur = 0.6 * jnp.exp(0.5 * jnp.tanh(0.5 * temper))
    excess = vapour - satur
    cloudy = 0.5 + sigmoid(third + excess)
    conden = 0.4 * jnp.tanh(excess) * cloudy
    autoconv = 0.3 * liquid * liquid * inverse(1.0 + liquid)
    evapor = 0.1 * rain_q * sigmoid(-excess)
    warmth = sigmoid(temper)
    freeze = 0.3 * liquid * (1.0 - warmth)
    melting = 0.2 * ice_q * warmth
    deposit = 0.35 * jnp.tanh(vapour - 0.8 * satur) * cloudy
    aggreg = 0.25 * ice_q * ice_q * inverse(1.0 + ice_q)
    falling = 0.5 * rain_q
    rolled = pltpu.roll(falling, 1, 0)
    level = lax.broadcasted_iota(jnp.int32, falling.shape, 0)
    from_above = jnp.where(level == 0, above, rolled)

    def choose(first, second, last):
        return jnp.where(warm, first, jnp.where(mixed, second, last))

    change = freeze - melting
    d_temp = choose(0.8 * (conden - evapor), 0.8 * conden + 0.5 * change, deposit + 0.5 * freeze)
    d_vapour = choose(evapor - conden, -conden, -deposit)
    d_liquid = choose(conden - autoconv, conden - freeze - autoconv, -freeze)
    d_rain = choose(autoconv - evapor, autoconv + melting, aggreg) + from_above - falling
    d_ice = choose(jnp.zeros_like(change), change, deposit + freeze - aggreg)
    after = tuple(
        value + 0.5 * delta
        for value, delta in zip(fields, (d_temp, d_vapour, d_liquid, d_rain, d_ice))
    )
    return after, rolled


def gather_moments(cfg, fetched, owner_col, rank_col, rank_row):
    levels = cfg["levels"]
    rows, stride = cfg["fetch_rows"], cfg["fetch_stride"]
    columns = owner_col.shape[0]
    place = lax.broadcasted_iota(jnp.int32, (columns, fetched.shape[0]), 1)
    main_at = owner_col * stride + rank_col
    rest_at = owner_col * stride + cfg["main"] + rank_col % rows
    pick = jnp.concatenate(
        [(place == main_at).astype(F32), (place == rest_at).astype(F32)], axis=0
    ).astype(BF16)
    high, low = split(fetched)
    both = jnp.dot(pick, jnp.concatenate([high, low], axis=1), preferred_element_type=F32)
    found = (both[:, :LANE] + both[:, LANE:]).T
    main, rest = found[:, :columns], found[:, columns:]
    size = cfg["fetch_rest"]
    total = jnp.zeros((size, columns), F32)
    for group in range(cfg["cap"] // rows):
        total = total + jnp.where(
            rank_row // rows == group, rest[group * size : (group + 1) * size], 0.0
        )
    third = main[:levels]
    first = jnp.concatenate([main[levels:], total], axis=0)
    return first, third


def physics_kernel(
    cfg,
    blocks,
    *refs,
):
    x_refs, refs = refs[:blocks], refs[blocks:]
    (
    fetched_ref,
    owner_col_ref,
    owner_row_ref,
    regime_ref,
    weights_ref,
    rows_ref,
    cols_ref,
    tend_ref,
    out_ref,
    a_ref,
    y_ref,
    ratio_ref,
    kappa_ref,
    energy_ref,
    third_ref,
    grad_ref,
    ) = refs
    levels, peers, cap = cfg["levels"], cfg["peers"], cfg["cap"]
    columns = blocks * LANE
    x_ref = [ref.reshape(levels * SUB, LANE) for ref in x_refs]
    a_ref, y_ref, ratio_ref = (blocks_of(ref, blocks) for ref in (a_ref, y_ref, ratio_ref))
    t_ref = tend_ref.reshape(levels * SUB, columns)

    owner_col, owner_row = owner_col_ref[...], owner_row_ref[...]
    same = owner_col == owner_row
    down = lax.broadcasted_iota(jnp.int32, (columns, columns), 0)
    across = lax.broadcasted_iota(jnp.int32, (columns, columns), 1)
    rank_row = jnp.sum((same & (down < across)).astype(F32), axis=0, keepdims=True).astype(jnp.int32)
    rank_col = jnp.sum((same & (across < down)).astype(F32), axis=1, keepdims=True).astype(jnp.int32)

    first, third = gather_moments(cfg, fetched_ref[...], owner_col, rank_col, rank_row)
    third_ref[...] = third
    below = jnp.concatenate([first[1:], first[-1:]], axis=0)
    energy_ref[...] = 0.5 + 60.0 * sigmoid(2.0 * (first + below))

    warm = regime_ref[...] == 0
    mixed = regime_ref[...] == 1

    def micro(tile, carry):
        base = tile * (SUB * SUB)
        fields = tuple(read_plane(x_ref, base + field, SUB, SUB) for field in range(5))
        moment = third_ref[pl.ds(pl.multiple_of(tile * SUB, SUB), SUB), :]
        above = []
        for step in range(MICRO_SUB):
            fields, rolled = micro_step(fields, moment, carry[step], warm, mixed)
            above.append(rolled)
        for field in range(5):
            write_plane(a_ref, base + field, SUB, fields[field])
        for field in range(5, SUB):
            write_plane(a_ref, base + field, SUB, read_plane(x_ref, base + field, SUB, SUB))
        return tuple(above)

    nothing = jnp.zeros((SUB, columns), F32)
    lax.fori_loop(0, levels // SUB, micro, (nothing,) * MICRO_SUB)

    pad = pl.ds(levels * SUB, SUB)
    write_tile(a_ref, pad, nothing)
    write_tile(y_ref, pad, nothing)
    kappa_tiles(cfg, a_ref, energy_ref, kappa_ref)
    solve(cfg, a_ref, kappa_ref, ratio_ref, y_ref)

    def again(_, carry):
        kappa_tiles(cfg, y_ref, energy_ref, kappa_ref)
        solve(cfg, a_ref, kappa_ref, ratio_ref, y_ref)
        return carry

    lax.fori_loop(1, TURB_ITERS, again, 0)

    last = pl.ds((levels - 1) * SUB, SUB)
    bottom, bottom_a = read_tile(y_ref, last), read_tile(a_ref, last)
    wind = jnp.sqrt(1.0 + bottom[5:6] * bottom[5:6] + bottom[6:7] * bottom[6:7])
    fluxes = jnp.concatenate(
        [
            -0.5 * wind * bottom[5:6],
            -0.5 * wind * bottom[6:7],
            0.5 * softplus(bottom_a[3:4]),
            -0.3 * wind * bottom[0:1],
        ],
        axis=0,
    )
    flux_high = fluxes.astype(BF16).astype(F32)
    doubled = jnp.concatenate([flux_high, fluxes - flux_high], axis=0)
    products = []
    for block in range(weights_ref.shape[0]):
        chosen = jnp.zeros((SUB, LANE), F32)
        for part in range(columns // LANE):
            chosen = jnp.where(
                cols_ref[block] == part, doubled[:, part * LANE : (part + 1) * LANE], chosen
            )
        high, low = split(weights_ref[block])
        wide = jnp.dot(
            chosen.astype(BF16), jnp.concatenate([high, low], axis=1), preferred_element_type=F32
        )
        once = wide[:, :LANE] + wide[:, LANE:]
        once = once + pltpu.roll(once, FLUX, 0)
        products.append(once)
    row_in = lax.broadcasted_iota(jnp.int32, (SUB, LANE), 0) // FLUX
    per_tile = SUB // FLUX
    ocean_at = 2 * cfg["main"] + SUB
    for peer in range(peers):
        for part in range(OBLK_DEV // per_tile):
            target = row_in + (peer * OBLK_DEV + part * per_tile)
            total = jnp.zeros((SUB, LANE), F32)
            for block, product in enumerate(products):
                total = total + jnp.where(target == rows_ref[block], product, 0.0)
            start = peer * cfg["back_stride"] + ocean_at + part * SUB
            out_ref[pl.ds(start, SUB), :] = total

    live = lax.broadcasted_iota(jnp.int32, (SUB, columns), 0) == SUB - 1
    for index, field in enumerate(GRAD_FIELDS):
        for tile in range(levels // SUB):
            here = tile * SUB * SUB + field
            drop = read_plane(y_ref, here, SUB, SUB) - read_plane(y_ref, here + SUB, SUB, SUB)
            if tile == levels // SUB - 1:
                ends = 1.0 if index == len(GRAD_FIELDS) - 1 else 0.0
                drop = jnp.where(live, ends, drop)
            grad_ref[pl.ds(index * levels + tile * SUB, SUB), :] = drop
    main, rows = cfg["main"], cfg["back_rows"]
    down = lax.broadcasted_iota(jnp.int32, (peers * main, columns), 0)
    put = (down == owner_row * main + rank_row).astype(F32).astype(BF16)
    down = lax.broadcasted_iota(jnp.int32, (peers * SUB, columns), 0)
    put_rest = (down == owner_row * SUB + rank_row % rows).astype(F32).astype(BF16)
    turn = (((1,), (1,)), ((), ()))

    def place(onehot, values):
        high, low = split(values)
        both = lax.dot_general(
            onehot, jnp.concatenate([high, low], axis=0), turn, preferred_element_type=F32
        )
        return both[:, :LANE] + both[:, LANE:]

    size = cfg["back_rest"]
    tail = grad_ref[pl.ds(2 * LANE, size), :]
    groups = cap // rows
    spread = jnp.concatenate(
        [jnp.where(rank_row // rows == group, tail, 0.0) for group in range(groups)], axis=0
    )
    sent = [
        (place(put, grad_ref[pl.ds(0, LANE), :]), 0, main),
        (place(put, grad_ref[pl.ds(LANE, LANE), :]), main, main),
        (place(put_rest, spread), 2 * main, SUB),
    ]
    for value, at, count in sent:
        for peer in range(peers):
            out_ref[pl.ds(peer * cfg["back_stride"] + at, count), :] = value[
                peer * count : (peer + 1) * count
            ]

    field_in = lax.broadcasted_iota(jnp.int32, (SUB, columns), 0)
    kept = (field_in >= 2) & (field_in < 5)
    for level in range(levels):
        cut = pl.ds(level * SUB, SUB)
        ended = jnp.where(kept, read_tile(a_ref, cut), read_tile(y_ref, cut))
        t_ref[cut, :] = ended - read_tile(x_ref, cut)


def update_kernel(cfg, moments_ref, back_ref, out_ref, ocean_ref, diff_ref):
    levels, peers, cap = cfg["levels"], cfg["peers"], cfg["cap"]
    stride, main = cfg["back_stride"], cfg["main"]
    count = len(GRAD_FIELDS) * levels
    block = pl.program_id(0)

    @pl.when(block == 0)
    def _():
        ocean_at = 2 * main + SUB
        total = back_ref[pl.ds(ocean_at, OBLK_DEV * FLUX), :]
        for peer in range(1, peers):
            total = total + back_ref[pl.ds(peer * stride + ocean_at, OBLK_DEV * FLUX), :]
        ocean_ref[...] = total

    width = LANE // peers
    for part in range(2):
        rows = [
            back_ref[pl.ds(part * main + block * width + slot, peers, stride=stride), :]
            for slot in range(width)
        ]
        diff_ref[pl.ds(SUB + part * LANE, LANE), :] = jnp.concatenate(rows, axis=0).T
    rows, size = cfg["back_rows"], cfg["back_rest"]
    turned = jnp.concatenate(
        [back_ref[pl.ds(2 * main + row, peers, stride=stride), :] for row in range(rows)], axis=0
    ).T
    tail = jnp.zeros((size, LANE), F32)
    for group in range(cap // rows):
        tail = jnp.where(block == group, turned[group * size : (group + 1) * size], tail)
    diff_ref[pl.ds(SUB + 2 * LANE, size), :] = tail
    diff_ref[pl.ds(0, SUB), :] = jnp.zeros((SUB, LANE), F32)

    m_ref = [moments_ref.reshape(levels * SUB, LANE)]
    o_ref = [out_ref.reshape(levels * SUB, LANE)]
    live = diff_ref[pl.ds(SUB + count - 1, 1), :] > 0.5
    row_in = lax.broadcasted_iota(jnp.int32, (SUB, LANE), 0)
    for tile in range(levels // SUB):
        grads = []
        for index in range(len(GRAD_FIELDS)):
            at = SUB + index * levels + tile * SUB
            here = diff_ref[pl.ds(at, SUB), :]
            if index == len(GRAD_FIELDS) - 1 and tile == levels // SUB - 1:
                here = jnp.where(row_in == SUB - 1, 0.0, here)
            grads.append(here + diff_ref[pl.ds(at - 1, SUB), :])
        grad_u, grad_v, grad_t, grad_q = grads
        production = [
            grad_u * grad_u + grad_v * grad_v,
            grad_t * grad_t,
            grad_q * grad_q,
            grad_t * grad_q,
            grad_u * grad_t,
            grad_v * grad_t,
            grad_u * grad_q,
            grad_u * grad_v,
        ]
        for index, value in enumerate(production):
            at = tile * SUB * SUB + index
            held = read_plane(m_ref, at, SUB, SUB)
            new = held + 0.5 * (jnp.tanh(value) - (0.3 + 0.1 * index) * held)
            write_plane(o_ref, at, SUB, jnp.where(live, new, held))


VMEM = pl.BlockSpec(memory_space=pltpu.VMEM)
SMEM = pl.BlockSpec(memory_space=pltpu.SMEM)


def pick_block(array, block):
    levels, fields, _ = array.shape
    return pl.BlockSpec((levels, fields, LANE), lambda _: (0, 0, block))


def local(state, span_owner, regime, moments, remap_weights, remap_rows, remap_cols):
    peers = lax.axis_size("node") * lax.axis_size("dev")
    levels, fields, columns = state.shape
    slots = moments.shape[2]
    blocks = columns // LANE
    cfg = plan(peers, slots // peers, levels)
    params = pltpu.CompilerParams(vmem_limit_bytes=48 * 1024 * 1024)

    packed = pl.pallas_call(
        functools.partial(pack_kernel, cfg),
        out_shape=jax.ShapeDtypeStruct((peers * cfg["fetch_stride"], LANE), F32),
        grid=(1,),
        in_specs=[pick_block(moments, block) for block in range(slots // LANE)],
        out_specs=VMEM,
        compiler_params=params,
    )(*[moments] * (slots // LANE))
    fetched = lax.all_to_all(packed, ("node", "dev"), split_axis=0, concat_axis=0, tiled=True)
    tendencies, outgoing = pl.pallas_call(
        functools.partial(physics_kernel, cfg, blocks),
        out_shape=(
            jax.ShapeDtypeStruct(state.shape, F32),
            jax.ShapeDtypeStruct((peers * cfg["back_stride"], LANE), F32),
        ),
        grid=(1,),
        in_specs=[pick_block(state, block) for block in range(blocks)] + [VMEM] * 5 + [SMEM] * 2,
        out_specs=(VMEM, VMEM),
        scratch_shapes=[
            pltpu.VMEM((blocks * (levels + 1) * fields, LANE), F32),
            pltpu.VMEM((blocks * (levels + 1) * fields, LANE), F32),
            pltpu.VMEM((blocks * levels * fields, LANE), F32),
            pltpu.VMEM((levels, columns), F32),
            pltpu.VMEM((levels, columns), F32),
            pltpu.VMEM((levels, columns), F32),
            pltpu.VMEM((len(GRAD_FIELDS) * levels, columns), F32),
        ],
        compiler_params=params,
    )(
        *[state] * blocks,
        fetched,
        span_owner,
        span_owner.reshape(1, columns),
        regime.reshape(1, columns),
        remap_weights,
        remap_rows,
        remap_cols,
    )
    back = lax.all_to_all(outgoing, ("node", "dev"), split_axis=0, concat_axis=0, tiled=True)
    moments_out, ocean = pl.pallas_call(
        functools.partial(update_kernel, cfg),
        out_shape=(
            jax.ShapeDtypeStruct(moments.shape, F32),
            jax.ShapeDtypeStruct((OBLK_DEV * FLUX, LANE), F32),
        ),
        grid=(slots // LANE,),
        in_specs=[pl.BlockSpec((levels, fields, LANE), lambda block: (0, 0, block)), VMEM],
        out_specs=(pl.BlockSpec((levels, fields, LANE), lambda block: (0, 0, block)), VMEM),
        scratch_shapes=[pltpu.VMEM((SUB + len(GRAD_FIELDS) * levels, LANE), F32)],
        compiler_params=params,
    )(moments, back)
    return (tendencies, moments_out, ocean.reshape(OBLK_DEV, FLUX, LANE))


def solution(mesh):
    return jax.shard_map(
        local,
        mesh=mesh,
        in_specs=(
            P(None, None, ("node", "dev")),
            P(("node", "dev"), None),
            P(("node", "dev")),
            P(None, None, ("node", "dev")),
            P(("node", "dev"), None, None),
            P(("node", "dev")),
            P(("node", "dev")),
        ),
        out_specs=(
            P(None, None, ("node", "dev")),
            P(None, None, ("node", "dev")),
            P(("node", "dev"), None, None),
        ),
        check_vma=False,
    )
```

time: 440 us -> 59 us (0.13)
  local copies, waits for them, and re-layouts: 220 us -> 1.43 us
  waiting for transfers between devices: 138 us -> 13.4 us
  other arithmetic: 45.7 us -> 0 us
  blocking collectives: 0 us -> 26.8 us
  between operations: 15.3 us -> 0.7 us
  starting transfers between devices: 16.6 us -> 7.3 us
  Pallas kernels: 0 us -> 9.15 us
    another operation x123 -> x0, local copies, waits for them, and re-layouts: 128 us -> none  [the longest x119 126 us: implicit(): return jnp.stack(solved_rows, axis=0)]
    unnamed x2 -> x0, waiting for transfers between devices: 125 us -> none
    sub x102 -> x0, local copies, waits for them, and re-layouts: 42.5 us -> none  [implicit(): y_now = d_rows[level] - c_rows[level][None, :] * y_next]
    all_to_all x0 -> x1, blocking collectives: none -> 26.8 us  [local(): lax.all_to_all(outgoing, ('node', 'dev'), split_axis=0, concat_axis=0, ti...]
    slice x30 -> x0, local copies, waits for them, and re-layouts: 20.3 us -> none  [the longest x8 9.25 us: level_grad(): padded = jnp.concatenate([field[:1], field, field[-1:]], axis=0)]
    unnamed x60 -> x17, local copies, waits for them, and re-layouts: 11.7 us -> 1.43 us
    add x7 -> x0, other arithmetic: 10.2 us -> none  [the longest x1 4.82 us: microphysics(): current[:, 4] + 0.5 * d_ice]
    all_to_all x3 -> x1, starting transfers between devices: 16.5 us -> 7.3 us  [local(): lax.all_to_all(packed, ('node', 'dev'), split_axis=0, concat_axis=0, tile...]
  transfers between devices with their start and end apart: 4 -> 1, of which waited for: 2 -> 1; matrix products, arithmetic and copies ran while one was open for 6% -> 0% of each run, Pallas kernels for 0% -> 0%
where the time goes in v1:
time: 59 us; the launch traced here: 58.8 us
  blocking collectives  26.8 us (45%)
  waiting for transfers between devices  13.4 us (23%)
  Pallas kernels  9.15 us (16%)
  starting transfers between devices  7.3 us (12%)
  local copies, waits for them, and re-layouts  1.43 us (2%)
  between operations  0.7 us (1%)
    all_to_all x1, blocking collectives, local(): lax.all_to_all(outgoing, ('node', 'dev'), split_axis=0, concat_axis=0, ti...  26.8 us
    all_to_all x1, waiting for transfers between devices, local(): lax.all_to_all(packed, ('node', 'dev'), split_axis=0, concat_axis=0, tile...  13.4 us
    all_to_all x1, starting transfers between devices, local(): lax.all_to_all(packed, ('node', 'dev'), split_axis=0, concat_axis=0, tile...  7.3 us
    pallas_call x1, Pallas kernels, local(): pl.pallas_call(functools.partial(physics_kernel, cfg, blocks), out_shape=...  5.93 us
    pallas_call x1, Pallas kernels, local(): pl.pallas_call(functools.partial(update_kernel, cfg), out_shape=(jax.Shap...  2.23 us
    unnamed x17, local copies, waits for them, and re-layouts  1.43 us
  transfers between devices with their start and end apart: 1, of which 1 were waited for; matrix products, arithmetic and copies ran while one was open for 0% of the time, Pallas kernels for 0%

profile of v1, /device:TPU:0, one launch (start us, length us, event | category | flops | bytes accessed | tf_op | source)
XLA Modules:
  0.0 58.8 jit_solution(11450918859321021079)
XLA Ops:
  0.6 0.0 copy-start
  0.6 1.3 %copy-done = f32[72,8,512]{2,1,0:T(8,128)S(1)} copy-done((f32[72,8,512]{2,1,0:T(8,128)S(1)}, f32[72,8,512]{2,1,0:T(8,128)}, u32[]{:S(2)}) %copy-start) | copy-done | bytes 1179672
  1.9 0.0 copy-start.4
  1.9 0.0 copy-start.3
  1.9 0.0 copy-start.5
  1.9 0.0 copy-start.6
  1.9 0.0 copy-start.7
  1.9 1.0 %shard_map.94 = f32[768,128]{1,0:T(8,128)} custom-call(f32[72,8,512]{2,1,0:T(8,128)S(1)} %copy-done, f32[72,8,512]{2,1,0:T(8,128)S(1)} %copy-done, f32[72,8,512]{2,1,0:T(8,128)S(1)} %copy-done, f32[72,8,512]{2,1,0:T(8,128)S(1)} %copy-done), custom_call_target="tpu_custom_call" | custom-call | tf_op jit(solution)/shard_map/pallas_call | solution.py:480
  2.9 0.0 copy-start.2
  2.9 7.3 %all-to-all-start = ((f32[32,24,128]{2,1,0:T(8,128)}), f32[32,24,128]{2,1,0:T(8,128)S(1)}, u32[]{:S(2)}, u32[]{:S(2)}) async-start(f32[32,24,128]{2,1,0:T(8,128)} %bitcast), calls=%async_computation | async-start | bytes 786432 | tf_op jit(solution)/shard_map/all_to_all | solution.py:488
  10.2 0.0 copy-done.4
  10.2 0.1 copy.10.refs_3_
  10.4 13.4 %all-to-all-done = f32[32,24,128]{2,1,0:T(8,128)S(1)} async-done(((f32[32,24,128]{2,1,0:T(8,128)}), f32[32,24,128]{2,1,0:T(8,128)S(1)}, u32[]{:S(2)}, u32[]{:S(2)}) %all-to-all-start) | async-done | bytes 393248 | tf_op jit(solution)/shard_map/all_to_all | solution.py:488
  23.8 0.0 copy-done.3
  23.8 0.0 copy-done.5
  23.8 0.0 copy-done.6
  23.8 0.0 copy-done.7
  23.8 0.0 copy-done.2
  23.8 5.9 %shard_map.95 = (f32[72,8,256]{2,1,0:T(8,128)}, f32[1792,128]{1,0:T(8,128)S(1)}) custom-call(f32[72,8,256]{2,1,0:T(8,128)S(1)} %copy-done.2, f32[72,8,256]{2,1,0:T(8,128)S(1)} %copy-done.2, f32[768,128]{1,0:T(8,128)S(1)} %bitcast.8, s32[256,1]{1,0:T(8,128)S(1)} %copy.10.refs_3_, s32[1,256]{1,0:T(1,128)S(1)} %bitcast.10, s32[1,256]{1,0:T(1,128)S(1)} %bitcast.11, ...), custom_call_target="tpu_custom_call" | custom-call | tf_op jit(solution)/shard_map/pallas_call | solution.py:489
  29.7 0.0 copy-start.1
  29.7 26.8 %all_to_all.22 = f32[32,56,128]{2,1,0:T(8,128)S(1)} all-to-all(f32[32,56,128]{2,1,0:T(8,128)S(1)} %bitcast.9), channel_id=1, replica_groups=mesh['node'=4,'dev'=8] {'node','dev'}, dimensions={0} | all-to-all | bytes 1835008 | tf_op jit(solution)/shard_map/all_to_all | solution.py:518
  56.5 0.0 copy-done.1
  56.5 2.2 %shard_map.96 = (f32[72,8,512]{2,1,0:T(8,128)}, f32[16,128]{1,0:T(8,128)}) custom-call(f32[72,8,512]{2,1,0:T(8,128)S(1)} %copy-done.1, f32[1792,128]{1,0:T(8,128)S(1)} %bitcast.7), custom_call_target="tpu_custom_call" | custom-call | tf_op jit(solution)/shard_map/pallas_call | solution.py:519
Async XLA Ops:
  0.6 1.3 %copy-start = (f32[72,8,512]{2,1,0:T(8,128)S(1)}, f32[72,8,512]{2,1,0:T(8,128)}, u32[]{:S(2)}) copy-start(f32[72,8,512]{2,1,0:T(8,128)} %moments_ref.1) | copy-start | bytes 3538948
  1.9 8.3 %copy-start.4 = (s32[256,1]{0,1:T(1,128)S(1)}, s32[256,1]{0,1:T(1,128)}, u32[]{:S(2)}) copy-start(s32[256,1]{0,1:T(1,128)} %param.8) | copy-start | bytes 3076
  1.9 21.9 %copy-start.3 = (f32[4,128,128]{2,1,0:T(8,128)S(1)}, f32[4,128,128]{2,1,0:T(8,128)}, u32[]{:S(2)}) copy-start(f32[4,128,128]{2,1,0:T(8,128)} %refs_6_.1) | copy-start | bytes 786436
  1.9 21.9 %copy-start.5 = (s32[256]{0:T(256)S(1)}, s32[256]{0:T(256)}, u32[]{:S(2)}) copy-start(s32[256]{0:T(256)} %param.9) | copy-start | bytes 3076
  1.9 21.9 %copy-start.6 = (s32[4]{0:T(128)S(1)}, s32[4]{0:T(128)}, u32[]{:S(2)}) copy-start(s32[4]{0:T(128)} %refs_7_.1) | copy-start | bytes 52
  1.9 21.9 %copy-start.7 = (s32[4]{0:T(128)S(1)}, s32[4]{0:T(128)}, u32[]{:S(2)}) copy-start(s32[4]{0:T(128)} %refs_8_.1) | copy-start | bytes 52
  2.9 20.9 %copy-start.2 = (f32[72,8,256]{2,1,0:T(8,128)S(1)}, f32[72,8,256]{2,1,0:T(8,128)}, u32[]{:S(2)}) copy-start(f32[72,8,256]{2,1,0:T(8,128)} %refs_1_.3) | copy-start | bytes 1769476
  2.9 20.8 %all-to-all-start = ((f32[32,24,128]{2,1,0:T(8,128)}), f32[32,24,128]{2,1,0:T(8,128)S(1)}, u32[]{:S(2)}, u32[]{:S(2)}) async-start(f32[32,24,128]{2,1,0:T(8,128)} %bitcast), calls=%async_computation | async-start | bytes 786432 | tf_op jit(solution)/shard_map/all_to_all | solution.py:488
  29.7 26.8 %copy-start.1 = (f32[72,8,512]{2,1,0:T(8,128)S(1)}, f32[72,8,512]{2,1,0:T(8,128)}, u32[]{:S(2)}) copy-start(f32[72,8,512]{2,1,0:T(8,128)} %moments_ref.1) | copy-start | bytes 3538948

commit v2 on v1

--- a/solution.py
+++ b/solution.py
@@ -34,7 +34,7 @@
         fetch_rows=fetch_rows,
         back_rows=back_rows,
         fetch_stride=main + SUB,
-        back_stride=2 * main + SUB + OBLK_DEV * FLUX,
+        back_stride=2 * main + SUB,
     )
 
 
@@ -81,11 +81,10 @@
         ref[cut, :] = value[:, block * LANE : (block + 1) * LANE]
 
 
-def pack_kernel(cfg, *refs):
+def pack(cfg, moment_refs, out_ref):
     levels, peers, cap = cfg["levels"], cfg["peers"], cfg["cap"]
     stride = cfg["fetch_stride"]
-    out_ref = refs[-1]
-    flat = [ref.reshape(levels * SUB, LANE) for ref in refs[:-1]]
+    flat = [ref.reshape(levels * SUB, LANE) for ref in moment_refs]
     first = read_plane(flat, 0, levels, SUB)
     third = read_plane(flat, 2, levels, SUB)
     cut = LANE - levels
@@ -211,16 +210,22 @@
     return after, rolled
 
 
-def gather_moments(cfg, fetched, owner_col, rank_col, rank_row):
-    levels = cfg["levels"]
+def one_hot_fetch(cfg, owner_col, rank_col):
     rows, stride = cfg["fetch_rows"], cfg["fetch_stride"]
     columns = owner_col.shape[0]
-    place = lax.broadcasted_iota(jnp.int32, (columns, fetched.shape[0]), 1)
+    place = lax.broadcasted_iota(jnp.int32, (columns, cfg["peers"] * stride), 1)
     main_at = owner_col * stride + rank_col
     rest_at = owner_col * stride + cfg["main"] + rank_col % rows
-    pick = jnp.concatenate(
+    return jnp.concatenate(
         [(place == main_at).astype(F32), (place == rest_at).astype(F32)], axis=0
     ).astype(BF16)
+
+
+def gather_moments(cfg, fetched, pick, rank_row):
+    levels, rows = cfg["levels"], cfg["fetch_rows"]
+    columns = rank_row.shape[1]
+    row_in = lax.broadcasted_iota(jnp.int32, fetched.shape, 0) % cfg["fetch_stride"]
+    fetched = jnp.where(row_in < cfg["main"] + rows, fetched, 0.0)
     high, low = split(fetched)
     both = jnp.dot(pick, jnp.concatenate([high, low], axis=1), preferred_element_type=F32)
     found = (both[:, :LANE] + both[:, LANE:]).T
@@ -236,30 +241,105 @@
     return first, third
 
 
-def physics_kernel(
-    cfg,
-    blocks,
-    *refs,
-):
+class Links:
+    def __init__(self):
+        self.nodes, self.devs = lax.axis_size("node"), lax.axis_size("dev")
+        self.node, self.dev = lax.axis_index("node"), lax.axis_index("dev")
+        self.me = self.node * self.devs + self.dev
+
+    def coordinates(self, peer):
+        return (peer // self.devs, peer % self.devs)
+
+
+def remote(source, target, sends, receives, step, where):
+    return pltpu.make_async_remote_copy(
+        src_ref=source,
+        dst_ref=target,
+        send_sem=sends.at[step],
+        recv_sem=receives.at[step],
+        device_id=where,
+        device_id_type=pl.DeviceIdType.MESH,
+    )
+
+
+def each(start, stop, body):
+    def step(index, carry):
+        body(index)
+        return carry
+
+    lax.fori_loop(start, stop, step, 0)
+
+
+def step_kernel(cfg, blocks, slot_blocks, *refs):
     x_refs, refs = refs[:blocks], refs[blocks:]
+    moment_refs, refs = refs[:slot_blocks], refs[slot_blocks:]
     (
-    fetched_ref,
-    owner_col_ref,
-    owner_row_ref,
-    regime_ref,
-    weights_ref,
-    rows_ref,
-    cols_ref,
-    tend_ref,
-    out_ref,
-    a_ref,
-    y_ref,
-    ratio_ref,
-    kappa_ref,
-    energy_ref,
-    third_ref,
-    grad_ref,
+        owner_col_ref,
+        owner_row_ref,
+        regime_ref,
+        weights_ref,
+        rows_ref,
+        cols_ref,
+        tend_ref,
+        back_ref,
+        ocean_ref,
+        packed_ref,
+        fetched_ref,
+        out_ref,
+        plane_ref,
+        plane_in_ref,
+        column_ref,
+        a_ref,
+        y_ref,
+        ratio_ref,
+        kappa_ref,
+        energy_ref,
+        third_ref,
+        grad_ref,
+        fetch_send,
+        fetch_recv,
+        back_send,
+        back_recv,
+        plane_send,
+        plane_recv,
+        column_send,
+        column_recv,
+        own_sem,
+        own_ocean_sem,
     ) = refs
+    links = Links()
+    me = links.me
+    barrier = pltpu.get_barrier_semaphore()
+    all_peers = cfg["peers"]
+
+    def greet(step):
+        pl.semaphore_signal(
+            barrier,
+            inc=1,
+            device_id=links.coordinates((me + step) % all_peers),
+            device_id_type=pl.DeviceIdType.MESH,
+        )
+
+    each(1, all_peers, greet)
+    pack(cfg, moment_refs, packed_ref)
+    pl.semaphore_wait(barrier, all_peers - 1)
+
+    def fetch_copy(step):
+        peer = (me + step) % all_peers
+        count = cfg["main"] + cfg["fetch_rows"]
+        return remote(
+            packed_ref.at[pl.ds(peer * cfg["fetch_stride"], count), :],
+            fetched_ref.at[pl.ds(me * cfg["fetch_stride"], count), :],
+            fetch_send,
+            fetch_recv,
+            step,
+            links.coordinates(peer),
+        )
+
+    each(1, all_peers, lambda step: fetch_copy(step).start())
+    own = pl.ds(pl.multiple_of(me * cfg["fetch_stride"], SUB), cfg["fetch_stride"])
+    fetched_ref[own, :] = packed_ref[own, :]
+
     levels, peers, cap = cfg["levels"], cfg["peers"], cfg["cap"]
     columns = blocks * LANE
     x_ref = [ref.reshape(levels * SUB, LANE) for ref in x_refs]
@@ -273,7 +353,9 @@
     rank_row = jnp.sum((same & (down < across)).astype(F32), axis=0, keepdims=True).astype(jnp.int32)
     rank_col = jnp.sum((same & (across < down)).astype(F32), axis=1, keepdims=True).astype(jnp.int32)
 
-    first, third = gather_moments(cfg, fetched_ref[...], owner_col, rank_col, rank_row)
+    pick = one_hot_fetch(cfg, owner_col, rank_col)
+    each(1, all_peers, lambda step: fetch_copy(step).wait_recv())
+    first, third = gather_moments(cfg, fetched_ref[...], pick, rank_row)
     third_ref[...] = third
     below = jnp.concatenate([first[1:], first[-1:]], axis=0)
     energy_ref[...] = 0.5 + 60.0 * sigmoid(2.0 * (first + below))
@@ -289,27 +371,24 @@
         for step in range(MICRO_SUB):
             fields, rolled = micro_step(fields, moment, carry[step], warm, mixed)
             above.append(rolled)
-        for field in range(5):
+        fields = fields + tuple(read_plane(x_ref, base + field, SUB, SUB) for field in (5, 6, 7))
+        for field in range(SUB):
             write_plane(a_ref, base + field, SUB, fields[field])
-        for field in range(5, SUB):
-            write_plane(a_ref, base + field, SUB, read_plane(x_ref, base + field, SUB, SUB))
+            write_plane(y_ref, base + field, SUB, fields[field])
         return tuple(above)
 
     nothing = jnp.zeros((SUB, columns), F32)
     lax.fori_loop(0, levels // SUB, micro, (nothing,) * MICRO_SUB)
 
     pad = pl.ds(levels * SUB, SUB)
-    write_tile(a_ref, pad, nothing)
     write_tile(y_ref, pad, nothing)
-    kappa_tiles(cfg, a_ref, energy_ref, kappa_ref)
-    solve(cfg, a_ref, kappa_ref, ratio_ref, y_ref)
 
     def again(_, carry):
         kappa_tiles(cfg, y_ref, energy_ref, kappa_ref)
         solve(cfg, a_ref, kappa_ref, ratio_ref, y_ref)
         return carry
 
-    lax.fori_loop(1, TURB_ITERS, again, 0)
+    lax.fori_loop(0, TURB_ITERS, again, 0)
 
     last = pl.ds((levels - 1) * SUB, SUB)
     bottom, bottom_a = read_tile(y_ref, last), read_tile(a_ref, last)
@@ -341,21 +420,42 @@
         products.append(once)
     row_in = lax.broadcasted_iota(jnp.int32, (SUB, LANE), 0) // FLUX
     per_tile = SUB // FLUX
-    ocean_at = 2 * cfg["main"] + SUB
-    for peer in range(peers):
-        for part in range(OBLK_DEV // per_tile):
-            target = row_in + (peer * OBLK_DEV + part * per_tile)
-            total = jnp.zeros((SUB, LANE), F32)
-            for block, product in enumerate(products):
-                total = total + jnp.where(target == rows_ref[block], product, 0.0)
-            start = peer * cfg["back_stride"] + ocean_at + part * SUB
-            out_ref[pl.ds(start, SUB), :] = total
+    share = OBLK_DEV * FLUX
+    floors = links.devs // 2
+    floor, side = links.dev // 2, links.dev % 2
+    group = links.nodes * 2
+    here = links.node * 2 + side
+    span = floors * share
+    for member in range(group):
+        for level in range(floors):
+            owner = member // 2 * links.devs + level * 2 + member % 2
+            for part in range(OBLK_DEV // per_tile):
+                target = row_in + (owner * OBLK_DEV + part * per_tile)
+                total = jnp.zeros((SUB, LANE), F32)
+                for block, product in enumerate(products):
+                    total = total + jnp.where(target == rows_ref[block], product, 0.0)
+                plane_ref[pl.ds(member * span + level * share + part * SUB, SUB), :] = total
+
+    def plane_copy(step):
+        member = (here + step) % group
+        return remote(
+            plane_ref.at[pl.ds(member * span, span), :],
+            plane_in_ref.at[pl.ds(here * span, span), :],
+            plane_send,
+            plane_recv,
+            step,
+            (member // 2, floor * 2 + member % 2),
+        )
+
+    each(1, group, lambda step: plane_copy(step).start())
+    mine = pl.ds(pl.multiple_of(here * span, SUB), span)
+    plane_in_ref[mine, :] = plane_ref[mine, :]
 
     live = lax.broadcasted_iota(jnp.int32, (SUB, columns), 0) == SUB - 1
     for index, field in enumerate(GRAD_FIELDS):
         for tile in range(levels // SUB):
-            here = tile * SUB * SUB + field
-            drop = read_plane(y_ref, here, SUB, SUB) - read_plane(y_ref, here + SUB, SUB, SUB)
+            at = tile * SUB * SUB + field
+            drop = read_plane(y_ref, at, SUB, SUB) - read_plane(y_ref, at + SUB, SUB, SUB)
             if tile == levels // SUB - 1:
                 ends = 1.0 if index == len(GRAD_FIELDS) - 1 else 0.0
                 drop = jnp.where(live, ends, drop)
@@ -391,6 +491,45 @@
                 peer * count : (peer + 1) * count
             ]
 
+    def back_copy(step):
+        peer = (me + step) % all_peers
+        count = 2 * main + rows
+        return remote(
+            out_ref.at[pl.ds(peer * cfg["back_stride"], count), :],
+            back_ref.at[pl.ds(me * cfg["back_stride"], count), :],
+            back_send,
+            back_recv,
+            step,
+            links.coordinates(peer),
+        )
+
+    each(1, all_peers, lambda step: back_copy(step).start())
+    own = pl.ds(pl.multiple_of(me * cfg["back_stride"], SUB), cfg["back_stride"])
+    own_copy = pltpu.make_async_copy(out_ref.at[own, :], back_ref.at[own, :], own_sem)
+    own_copy.start()
+
+    each(1, group, lambda step: plane_copy(step).wait_recv())
+    total = plane_in_ref[pl.ds(0, span), :]
+    for member in range(1, group):
+        total = total + plane_in_ref[pl.ds(member * span, span), :]
+    column_ref[...] = total
+
+    def column_copy(step):
+        level = (floor + step) % floors
+        return remote(
+            column_ref.at[pl.ds(level * share, share), :],
+            ocean_ref.at[pl.ds(floor * share, share), :],
+            column_send,
+            column_recv,
+            step,
+            (links.node, level * 2 + side),
+        )
+
+    each(1, floors, lambda step: column_copy(step).start())
+    mine = pl.ds(pl.multiple_of(floor * share, SUB), share)
+    own_ocean = pltpu.make_async_copy(column_ref.at[mine, :], ocean_ref.at[mine, :], own_ocean_sem)
+    own_ocean.start()
+
     field_in = lax.broadcasted_iota(jnp.int32, (SUB, columns), 0)
     kept = (field_in >= 2) & (field_in < 5)
     for level in range(levels):
@@ -398,8 +537,15 @@
         ended = jnp.where(kept, read_tile(a_ref, cut), read_tile(y_ref, cut))
         t_ref[cut, :] = ended - read_tile(x_ref, cut)
 
-
-def update_kernel(cfg, moments_ref, back_ref, out_ref, ocean_ref, diff_ref):
+    own_copy.wait()
+    own_ocean.wait()
+    each(1, all_peers, lambda step: fetch_copy(step).wait_send())
+    each(1, group, lambda step: plane_copy(step).wait_send())
+    each(1, floors, lambda step: column_copy(step).wait())
+    each(1, all_peers, lambda step: back_copy(step).wait())
+
+
+def update_kernel(cfg, moments_ref, back_ref, parts_ref, out_ref, ocean_ref, diff_ref):
     levels, peers, cap = cfg["levels"], cfg["peers"], cfg["cap"]
     stride, main = cfg["back_stride"], cfg["main"]
     count = len(GRAD_FIELDS) * levels
@@ -407,10 +553,10 @@
 
     @pl.when(block == 0)
     def _():
-        ocean_at = 2 * main + SUB
-        total = back_ref[pl.ds(ocean_at, OBLK_DEV * FLUX), :]
-        for peer in range(1, peers):
-            total = total + back_ref[pl.ds(peer * stride + ocean_at, OBLK_DEV * FLUX), :]
+        share = OBLK_DEV * FLUX
+        total = parts_ref[pl.ds(0, share), :]
+        for floor in range(1, parts_ref.shape[0] // share):
+            total = total + parts_ref[pl.ds(floor * share, share), :]
         ocean_ref[...] = total
 
     width = LANE // peers
@@ -477,37 +623,56 @@
     cfg = plan(peers, slots // peers, levels)
     params = pltpu.CompilerParams(vmem_limit_bytes=48 * 1024 * 1024)
 
-    packed = pl.pallas_call(
-        functools.partial(pack_kernel, cfg),
-        out_shape=jax.ShapeDtypeStruct((peers * cfg["fetch_stride"], LANE), F32),
-        grid=(1,),
-        in_specs=[pick_block(moments, block) for block in range(slots // LANE)],
-        out_specs=VMEM,
-        compiler_params=params,
-    )(*[moments] * (slots // LANE))
-    fetched = lax.all_to_all(packed, ("node", "dev"), split_axis=0, concat_axis=0, tiled=True)
-    tendencies, outgoing = pl.pallas_call(
-        functools.partial(physics_kernel, cfg, blocks),
+    floors = lax.axis_size("dev") // 2
+    group = 2 * lax.axis_size("node")
+    share = OBLK_DEV * FLUX
+    whole = pl.BlockSpec(memory_space=pl.ANY)
+
+    def rows_of(count):
+        return pltpu.VMEM((count, LANE), F32)
+
+    def copies_of(count):
+        return [pltpu.SemaphoreType.DMA((count,))] * 2
+
+    tendencies, back, parts = pl.pallas_call(
+        functools.partial(step_kernel, cfg, blocks, slots // LANE),
         out_shape=(
             jax.ShapeDtypeStruct(state.shape, F32),
             jax.ShapeDtypeStruct((peers * cfg["back_stride"], LANE), F32),
+            jax.ShapeDtypeStruct((floors * share, LANE), F32),
         ),
         grid=(1,),
-        in_specs=[pick_block(state, block) for block in range(blocks)] + [VMEM] * 5 + [SMEM] * 2,
-        out_specs=(VMEM, VMEM),
+        in_specs=[pick_block(state, block) for block in range(blocks)]
+        + [pick_block(moments, block) for block in range(slots // LANE)]
+        + [VMEM] * 4
+        + [SMEM] * 2,
+        out_specs=(VMEM, whole, whole),
         scratch_shapes=[
-            pltpu.VMEM((blocks * (levels + 1) * fields, LANE), F32),
-            pltpu.VMEM((blocks * (levels + 1) * fields, LANE), F32),
-            pltpu.VMEM((blocks * levels * fields, LANE), F32),
+            rows_of(peers * cfg["fetch_stride"]),
+            rows_of(peers * cfg["fetch_stride"]),
+            rows_of(peers * cfg["back_stride"]),
+            rows_of(group * floors * share),
+            rows_of(group * floors * share),
+            rows_of(floors * share),
+            rows_of(blocks * (levels + 1) * fields),
+            rows_of(blocks * (levels + 1) * fields),
+            rows_of(blocks * levels * fields),
             pltpu.VMEM((levels, columns), F32),
             pltpu.VMEM((levels, columns), F32),
             pltpu.VMEM((levels, columns), F32),
             pltpu.VMEM((len(GRAD_FIELDS) * levels, columns), F32),
-        ],
-        compiler_params=params,
+        ]
+        + copies_of(peers)
+        + copies_of(peers)
+        + copies_of(group)
+        + copies_of(floors)
+        + [pltpu.SemaphoreType.DMA, pltpu.SemaphoreType.DMA],
+        compiler_params=pltpu.CompilerParams(
+            vmem_limit_bytes=48 * 1024 * 1024, collective_id=0, has_side_effects=True
+        ),
     )(
         *[state] * blocks,
-        fetched,
+        *[moments] * (slots // LANE),
         span_owner,
         span_owner.reshape(1, columns),
         regime.reshape(1, columns),
@@ -515,7 +680,6 @@
         remap_rows,
         remap_cols,
     )
-    back = lax.all_to_all(outgoing, ("node", "dev"), split_axis=0, concat_axis=0, tiled=True)
     moments_out, ocean = pl.pallas_call(
         functools.partial(update_kernel, cfg),
         out_shape=(
@@ -523,11 +687,11 @@
             jax.ShapeDtypeStruct((OBLK_DEV * FLUX, LANE), F32),
         ),
         grid=(slots // LANE,),
-        in_specs=[pl.BlockSpec((levels, fields, LANE), lambda block: (0, 0, block)), VMEM],
+        in_specs=[pl.BlockSpec((levels, fields, LANE), lambda block: (0, 0, block)), VMEM, VMEM],
         out_specs=(pl.BlockSpec((levels, fields, LANE), lambda block: (0, 0, block)), VMEM),
         scratch_shapes=[pltpu.VMEM((SUB + len(GRAD_FIELDS) * levels, LANE), F32)],
         compiler_params=params,
-    )(moments, back)
+    )(moments, back, parts)
     return (tendencies, moments_out, ocean.reshape(OBLK_DEV, FLUX, LANE))
 
 

time: 59 us -> 48.2 us (0.82)
  Pallas kernels: 9.15 us -> 39.7 us
  blocking collectives: 26.8 us -> 0 us
  waiting for transfers between devices: 13.4 us -> 0 us
  starting transfers between devices: 7.3 us -> 0 us
  local copies, waits for them, and re-layouts: 1.43 us -> 7.57 us
    pallas_call x2 -> x1, Pallas kernels: 6.92 us -> 37.5 us  [local(): pl.pallas_call(functools.partial(step_kernel, cfg, blocks, slots // LANE)...]
    all_to_all x1 -> x0, blocking collectives: 26.8 us -> none  [local(): lax.all_to_all(outgoing, ('node', 'dev'), split_axis=0, concat_axis=0, ti...]
    all_to_all x1 -> x0, waiting for transfers between devices: 13.4 us -> none  [local(): lax.all_to_all(packed, ('node', 'dev'), split_axis=0, concat_axis=0, tile...]
    all_to_all x1 -> x0, starting transfers between devices: 7.3 us -> none  [local(): lax.all_to_all(packed, ('node', 'dev'), split_axis=0, concat_axis=0, tile...]
    unnamed x17 -> x18, local copies, waits for them, and re-layouts: 1.43 us -> 7.57 us
  transfers between devices with their start and end apart: 1 -> 0, of which waited for: 1 -> 0; matrix products, arithmetic and copies ran while one was open for 0% -> 0% of each run, Pallas kernels for 0% -> 0%
where the time goes in v2:
time: 48.2 us; the launch traced here: 47.9 us
  Pallas kernels  39.7 us (82%)
  local copies, waits for them, and re-layouts  7.57 us (16%)
  between operations  0.67 us (1%)
    pallas_call x1, Pallas kernels, local(): pl.pallas_call(functools.partial(step_kernel, cfg, blocks, slots // LANE)...  37.5 us
    unnamed x18, local copies, waits for them, and re-layouts  7.57 us
    pallas_call x1, Pallas kernels, local(): pl.pallas_call(functools.partial(update_kernel, cfg), out_shape=(jax.Shap...  2.21 us

profile of v2, /device:TPU:0, one launch (start us, length us, event | category | flops | bytes accessed | tf_op | source)
XLA Modules:
  0.0 47.9 jit_solution(9556249535068788957)
XLA Ops:
  0.6 0.8 %copy.10.refs_6_ = s32[256,1]{1,0:T(8,128)S(1)} copy(s32[256,1]{0,1:T(1,128)} %param.8) | data formatting | bytes 2048 | tf_op args[1]
  1.4 0.0 copy-start
  1.5 1.3 %copy-done = f32[72,8,512]{2,1,0:T(8,128)S(1)} copy-done((f32[72,8,512]{2,1,0:T(8,128)S(1)}, f32[72,8,512]{2,1,0:T(8,128)}, u32[]{:S(2)}) %copy-start) | copy-done | bytes 1179672
  2.7 0.0 copy-start.2
  2.7 1.1 %copy-done.2 = f32[72,8,256]{2,1,0:T(8,128)S(1)} copy-done((f32[72,8,256]{2,1,0:T(8,128)S(1)}, f32[72,8,256]{2,1,0:T(8,128)}, u32[]{:S(2)}) %copy-start.2) | copy-done | bytes 589848
  3.8 0.0 copy-start.3
  3.8 0.9 %copy-done.3 = f32[4,128,128]{2,1,0:T(8,128)S(1)} copy-done((f32[4,128,128]{2,1,0:T(8,128)S(1)}, f32[4,128,128]{2,1,0:T(8,128)}, u32[]{:S(2)}) %copy-start.3) | copy-done | bytes 262168
  4.7 0.0 copy-start.4
  4.7 0.7 %copy-done.4 = s32[256,1]{0,1:T(1,128)S(1)} copy-done((s32[256,1]{0,1:T(1,128)S(1)}, s32[256,1]{0,1:T(1,128)}, u32[]{:S(2)}) %copy-start.4) | copy-done | bytes 1048
  5.4 0.0 copy-start.5
  5.4 0.7 %copy-done.5 = s32[256]{0:T(256)S(1)} copy-done((s32[256]{0:T(256)S(1)}, s32[256]{0:T(256)}, u32[]{:S(2)}) %copy-start.5) | copy-done | bytes 1048
  6.1 0.0 copy-start.6
  6.1 0.7 %copy-done.6 = s32[4]{0:T(128)S(1)} copy-done((s32[4]{0:T(128)S(1)}, s32[4]{0:T(128)}, u32[]{:S(2)}) %copy-start.6) | copy-done | bytes 40
  6.8 0.0 copy-start.7
  6.8 0.7 %copy-done.7 = s32[4]{0:T(128)S(1)} copy-done((s32[4]{0:T(128)S(1)}, s32[4]{0:T(128)}, u32[]{:S(2)}) %copy-start.7) | copy-done | bytes 40
  7.4 0.0 copy-start.1
  7.4 37.5 %shard_map.94 = (f32[72,8,256]{2,1,0:T(8,128)S(1)}, f32[1280,128]{1,0:T(8,128)S(1)}, f32[64,128]{1,0:T(8,128)S(1)}) custom-call(f32[72,8,256]{2,1,0:T(8,128)S(1)} %copy-done.2, f32[72,8,256]{2,1,0:T(8,128)S(1)} %copy-done.2, f32[72,8,512]{2,1,0:T(8,128)S(1)} %copy-done, f32[72,8,512]{2,1,0:T(8,128)S(1)} %copy-done, f32[72,8,512]{2,1,0:T(8,128)S(1)} %copy-done, ...), custom_call_target="tpu_custom_call" | custom-call | tf_op jit(solution)/shard_map/pallas_call | solution.py:637
  44.9 0.0 copy-done.1
  44.9 2.2 %shard_map.95 = (f32[72,8,512]{2,1,0:T(8,128)}, f32[16,128]{1,0:T(8,128)}) custom-call(f32[72,8,512]{2,1,0:T(8,128)S(1)} %copy-done.1, f32[1280,128]{1,0:T(8,128)S(1)} %get-tuple-element.9.back_ref, f32[64,128]{1,0:T(8,128)S(1)} %get-tuple-element.10.parts_ref), custom_call_target="tpu_custom_call" | custom-call | tf_op jit(solution)/shard_map/pallas_call | solution.py:683
  47.1 0.8 %copy.12 = f32[72,8,256]{2,1,0:T(8,128)} copy(f32[72,8,256]{2,1,0:T(8,128)S(1)} %get-tuple-element.16) | data formatting | bytes 1179648
Async XLA Ops:
  1.4 1.3 %copy-start = (f32[72,8,512]{2,1,0:T(8,128)S(1)}, f32[72,8,512]{2,1,0:T(8,128)}, u32[]{:S(2)}) copy-start(f32[72,8,512]{2,1,0:T(8,128)} %moments_ref.1) | copy-start | bytes 3538948
  2.7 1.1 %copy-start.2 = (f32[72,8,256]{2,1,0:T(8,128)S(1)}, f32[72,8,256]{2,1,0:T(8,128)}, u32[]{:S(2)}) copy-start(f32[72,8,256]{2,1,0:T(8,128)} %refs_1_.1) | copy-start | bytes 1769476
  3.8 0.9 %copy-start.3 = (f32[4,128,128]{2,1,0:T(8,128)S(1)}, f32[4,128,128]{2,1,0:T(8,128)}, u32[]{:S(2)}) copy-start(f32[4,128,128]{2,1,0:T(8,128)} %refs_9_.1) | copy-start | bytes 786436
  4.7 0.7 %copy-start.4 = (s32[256,1]{0,1:T(1,128)S(1)}, s32[256,1]{0,1:T(1,128)}, u32[]{:S(2)}) copy-start(s32[256,1]{0,1:T(1,128)} %param.8) | copy-start | bytes 3076
  5.4 0.7 %copy-start.5 = (s32[256]{0:T(256)S(1)}, s32[256]{0:T(256)}, u32[]{:S(2)}) copy-start(s32[256]{0:T(256)} %param.9) | copy-start | bytes 3076
  6.1 0.7 %copy-start.6 = (s32[4]{0:T(128)S(1)}, s32[4]{0:T(128)}, u32[]{:S(2)}) copy-start(s32[4]{0:T(128)} %refs_10_.1) | copy-start | bytes 52
  6.8 0.7 %copy-start.7 = (s32[4]{0:T(128)S(1)}, s32[4]{0:T(128)}, u32[]{:S(2)}) copy-start(s32[4]{0:T(128)} %refs_11_.1) | copy-start | bytes 52
  7.4 37.5 %copy-start.1 = (f32[72,8,512]{2,1,0:T(8,128)S(1)}, f32[72,8,512]{2,1,0:T(8,128)}, u32[]{:S(2)}) copy-start(f32[72,8,512]{2,1,0:T(8,128)} %moments_ref.1) | copy-start | bytes 3538948

commit v3 on v2

--- a/solution.py
+++ b/solution.py
@@ -13,6 +13,7 @@
 LANE = 128
 SUB = 8
 FLUX = 4
+VMEM_BYTES = 60 * 1024 * 1024
 GRAD_FIELDS = (5, 6, 0, 1)
 F32 = jnp.float32
 BF16 = jnp.bfloat16
@@ -81,10 +82,9 @@
         ref[cut, :] = value[:, block * LANE : (block + 1) * LANE]
 
 
-def pack(cfg, moment_refs, out_ref):
+def pack(cfg, flat, out_ref):
     levels, peers, cap = cfg["levels"], cfg["peers"], cfg["cap"]
     stride = cfg["fetch_stride"]
-    flat = [ref.reshape(levels * SUB, LANE) for ref in moment_refs]
     first = read_plane(flat, 0, levels, SUB)
     third = read_plane(flat, 2, levels, SUB)
     cut = LANE - levels
@@ -175,39 +175,53 @@
         write_tile(y_ref, tile(level), lower)
 
 
-def micro_step(fields, third, above, warm, mixed):
+def micro_rates(fields, above, warm, mixed):
     temper, raw_v, raw_c, raw_r, raw_i = fields
     vapour, liquid, rain_q, ice_q = (softplus(raw) for raw in (raw_v, raw_c, raw_r, raw_i))
     satur = 0.6 * jnp.exp(0.5 * jnp.tanh(0.5 * temper))
     excess = vapour - satur
-    cloudy = 0.5 + sigmoid(third + excess)
-    conden = 0.4 * jnp.tanh(excess) * cloudy
     autoconv = 0.3 * liquid * liquid * inverse(1.0 + liquid)
     evapor = 0.1 * rain_q * sigmoid(-excess)
     warmth = sigmoid(temper)
     freeze = 0.3 * liquid * (1.0 - warmth)
     melting = 0.2 * ice_q * warmth
-    deposit = 0.35 * jnp.tanh(vapour - 0.8 * satur) * cloudy
     aggreg = 0.25 * ice_q * ice_q * inverse(1.0 + ice_q)
     falling = 0.5 * rain_q
     rolled = pltpu.roll(falling, 1, 0)
     level = lax.broadcasted_iota(jnp.int32, falling.shape, 0)
     from_above = jnp.where(level == 0, above, rolled)
+    liquid_phase = warm | mixed
 
     def choose(first, second, last):
         return jnp.where(warm, first, jnp.where(mixed, second, last))
 
     change = freeze - melting
-    d_temp = choose(0.8 * (conden - evapor), 0.8 * conden + 0.5 * change, deposit + 0.5 * freeze)
-    d_vapour = choose(evapor - conden, -conden, -deposit)
-    d_liquid = choose(conden - autoconv, conden - freeze - autoconv, -freeze)
+    zero = jnp.zeros_like(change)
+    d_temp = choose(-0.8 * evapor, 0.5 * change, 0.5 * freeze)
+    d_vapour = jnp.where(warm, evapor, 0.0)
+    d_liquid = -choose(autoconv, freeze + autoconv, freeze)
     d_rain = choose(autoconv - evapor, autoconv + melting, aggreg) + from_above - falling
-    d_ice = choose(jnp.zeros_like(change), change, deposit + freeze - aggreg)
+    d_ice = choose(zero, change, freeze - aggreg)
     after = tuple(
         value + 0.5 * delta
         for value, delta in zip(fields, (d_temp, d_vapour, d_liquid, d_rain, d_ice))
     )
-    return after, rolled
+    factor = jnp.where(liquid_phase, 0.4, 0.35) * jnp.tanh(
+        vapour - jnp.where(liquid_phase, 1.0, 0.8) * satur
+    )
+    return after, factor, excess, rolled
+
+
+def micro_cloud(after, factor, excess, third, icy):
+    temper, raw_v, raw_c, raw_r, raw_i = after
+    change = 0.5 * factor * (0.5 + sigmoid(third + excess))
+    return (
+        temper + jnp.where(icy, 1.0, 0.8) * change,
+        raw_v - change,
+        raw_c + jnp.where(icy, 0.0, change),
+        raw_r,
+        raw_i + jnp.where(icy, change, 0.0),
+    )
 
 
 def one_hot_fetch(cfg, owner_col, rank_col):
@@ -271,18 +285,24 @@
 
 
 def step_kernel(cfg, blocks, slot_blocks, *refs):
-    x_refs, refs = refs[:blocks], refs[blocks:]
-    moment_refs, refs = refs[:slot_blocks], refs[slot_blocks:]
     (
-        owner_col_ref,
+        state_ref,
+        moments_ref,
         owner_row_ref,
         regime_ref,
-        weights_ref,
+        weights_in_ref,
         rows_ref,
         cols_ref,
-        tend_ref,
+        mixed_ref,
         back_ref,
         ocean_ref,
+        x_buf,
+        m_buf,
+        weights_ref,
+        early_ref,
+        pick_ref,
+        put_ref,
+        put_rest_ref,
         packed_ref,
         fetched_ref,
         out_ref,
@@ -290,7 +310,7 @@
         plane_in_ref,
         column_ref,
         a_ref,
-        y_ref,
+        y_buf,
         ratio_ref,
         kappa_ref,
         energy_ref,
@@ -306,7 +326,26 @@
         column_recv,
         own_sem,
         own_ocean_sem,
+        x_sem,
+        m_sem,
+        weights_sem,
+        mixed_sem,
     ) = refs
+    levels = cfg["levels"]
+
+    def block_copies(source, target, sems, count):
+        return [
+            pltpu.make_async_copy(
+                source.at[:, :, pl.ds(block * LANE, LANE)], target.at[block], sems.at[block]
+            )
+            for block in range(count)
+        ]
+
+    m_copies = block_copies(moments_ref, m_buf, m_sem, slot_blocks)
+    x_copies = block_copies(state_ref, x_buf, x_sem, blocks)
+    weights_copy = pltpu.make_async_copy(weights_in_ref, weights_ref, weights_sem)
+    for copy in m_copies + x_copies + [weights_copy]:
+        copy.start()
     links = Links()
     me = links.me
     barrier = pltpu.get_barrier_semaphore()
@@ -321,7 +360,10 @@
         )
 
     each(1, all_peers, greet)
-    pack(cfg, moment_refs, packed_ref)
+    for copy in m_copies:
+        copy.wait()
+    flat_moments = m_buf.reshape(slot_blocks * levels * SUB, LANE)
+    pack(cfg, blocks_of(flat_moments, slot_blocks), packed_ref)
     pl.semaphore_wait(barrier, all_peers - 1)
 
     def fetch_copy(step):
@@ -342,46 +384,77 @@
 
     levels, peers, cap = cfg["levels"], cfg["peers"], cfg["cap"]
     columns = blocks * LANE
-    x_ref = [ref.reshape(levels * SUB, LANE) for ref in x_refs]
-    a_ref, y_ref, ratio_ref = (blocks_of(ref, blocks) for ref in (a_ref, y_ref, ratio_ref))
-    t_ref = tend_ref.reshape(levels * SUB, columns)
-
-    owner_col, owner_row = owner_col_ref[...], owner_row_ref[...]
+    x_ref = blocks_of(x_buf.reshape(blocks * levels * SUB, LANE), blocks)
+    y_ref = blocks_of(y_buf.reshape(blocks * (levels + 1) * SUB, LANE), blocks)
+    a_ref, ratio_ref = blocks_of(a_ref, blocks), blocks_of(ratio_ref, blocks)
+
+    def as_column(row):
+        wide = jnp.broadcast_to(row.astype(F32), (LANE, columns)).T
+        return wide[:, :1].astype(jnp.int32)
+
+    owner_row = owner_row_ref[...]
+    owner_col = as_column(owner_row)
     same = owner_col == owner_row
     down = lax.broadcasted_iota(jnp.int32, (columns, columns), 0)
     across = lax.broadcasted_iota(jnp.int32, (columns, columns), 1)
     rank_row = jnp.sum((same & (down < across)).astype(F32), axis=0, keepdims=True).astype(jnp.int32)
-    rank_col = jnp.sum((same & (across < down)).astype(F32), axis=1, keepdims=True).astype(jnp.int32)
-
-    pick = one_hot_fetch(cfg, owner_col, rank_col)
+    rank_col = as_column(rank_row)
+    pick_ref[...] = one_hot_fetch(cfg, owner_col, rank_col)
+    main, rows = cfg["main"], cfg["back_rows"]
+    down = lax.broadcasted_iota(jnp.int32, (peers * main, columns), 0)
+    put_ref[...] = (down == owner_row * main + rank_row).astype(F32).astype(BF16)
+    down = lax.broadcasted_iota(jnp.int32, (peers * SUB, columns), 0)
+    put_rest_ref[...] = (down == owner_row * SUB + rank_row % rows).astype(F32).astype(BF16)
+
+    warm = regime_ref[...] == 0
+    mixed = regime_ref[...] == 1
+    icy = regime_ref[...] == 2
+    for copy in x_copies:
+        copy.wait()
+
+    def tile_rows(tile, plane):
+        return pl.ds(pl.multiple_of(plane * levels + tile * SUB, SUB), SUB)
+
+    def micro_early(tile, above):
+        base = tile * (SUB * SUB)
+        fields = tuple(read_plane(x_ref, base + field, SUB, SUB) for field in range(5))
+        after, factor, excess, rolled = micro_rates(fields, above, warm, mixed)
+        for plane, value in enumerate(after + (factor, excess)):
+            early_ref[tile_rows(tile, plane), :] = value
+        for field in (5, 6, 7):
+            value = read_plane(x_ref, base + field, SUB, SUB)
+            write_plane(a_ref, base + field, SUB, value)
+            write_plane(y_ref, base + field, SUB, value)
+        return rolled
+
+    nothing = jnp.zeros((SUB, columns), F32)
+    lax.fori_loop(0, levels // SUB, micro_early, nothing)
+    pad = pl.ds(levels * SUB, SUB)
+    write_tile(y_ref, pad, nothing)
+    weights_copy.wait()
+
     each(1, all_peers, lambda step: fetch_copy(step).wait_recv())
-    first, third = gather_moments(cfg, fetched_ref[...], pick, rank_row)
+    first, third = gather_moments(cfg, fetched_ref[...], pick_ref[...], rank_row)
     third_ref[...] = third
     below = jnp.concatenate([first[1:], first[-1:]], axis=0)
     energy_ref[...] = 0.5 + 60.0 * sigmoid(2.0 * (first + below))
 
-    warm = regime_ref[...] == 0
-    mixed = regime_ref[...] == 1
-
     def micro(tile, carry):
         base = tile * (SUB * SUB)
-        fields = tuple(read_plane(x_ref, base + field, SUB, SUB) for field in range(5))
-        moment = third_ref[pl.ds(pl.multiple_of(tile * SUB, SUB), SUB), :]
-        above = []
-        for step in range(MICRO_SUB):
-            fields, rolled = micro_step(fields, moment, carry[step], warm, mixed)
-            above.append(rolled)
-        fields = fields + tuple(read_plane(x_ref, base + field, SUB, SUB) for field in (5, 6, 7))
-        for field in range(SUB):
+        early = tuple(early_ref[tile_rows(tile, plane), :] for plane in range(7))
+        moment = third_ref[tile_rows(tile, 0), :]
+        fields = micro_cloud(early[:5], early[5], early[6], moment, icy)
+        below = []
+        for above in carry:
+            after, factor, excess, rolled = micro_rates(fields, above, warm, mixed)
+            fields = micro_cloud(after, factor, excess, moment, icy)
+            below.append(rolled)
+        for field in range(5):
             write_plane(a_ref, base + field, SUB, fields[field])
             write_plane(y_ref, base + field, SUB, fields[field])
-        return tuple(above)
-
-    nothing = jnp.zeros((SUB, columns), F32)
-    lax.fori_loop(0, levels // SUB, micro, (nothing,) * MICRO_SUB)
-
-    pad = pl.ds(levels * SUB, SUB)
-    write_tile(y_ref, pad, nothing)
+        return tuple(below)
+
+    lax.fori_loop(0, levels // SUB, micro, (nothing,) * (MICRO_SUB - 1))
 
     def again(_, carry):
         kappa_tiles(cfg, y_ref, energy_ref, kappa_ref)
@@ -460,11 +533,6 @@
                 ends = 1.0 if index == len(GRAD_FIELDS) - 1 else 0.0
                 drop = jnp.where(live, ends, drop)
             grad_ref[pl.ds(index * levels + tile * SUB, SUB), :] = drop
-    main, rows = cfg["main"], cfg["back_rows"]
-    down = lax.broadcasted_iota(jnp.int32, (peers * main, columns), 0)
-    put = (down == owner_row * main + rank_row).astype(F32).astype(BF16)
-    down = lax.broadcasted_iota(jnp.int32, (peers * SUB, columns), 0)
-    put_rest = (down == owner_row * SUB + rank_row % rows).astype(F32).astype(BF16)
     turn = (((1,), (1,)), ((), ()))
 
     def place(onehot, values):
@@ -481,9 +549,9 @@
         [jnp.where(rank_row // rows == group, tail, 0.0) for group in range(groups)], axis=0
     )
     sent = [
-        (place(put, grad_ref[pl.ds(0, LANE), :]), 0, main),
-        (place(put, grad_ref[pl.ds(LANE, LANE), :]), main, main),
-        (place(put_rest, spread), 2 * main, SUB),
+        (place(put_ref[...], grad_ref[pl.ds(0, LANE), :]), 0, main),
+        (place(put_ref[...], grad_ref[pl.ds(LANE, LANE), :]), main, main),
+        (place(put_rest_ref[...], spread), 2 * main, SUB),
     ]
     for value, at, count in sent:
         for peer in range(peers):
@@ -530,13 +598,23 @@
     own_ocean = pltpu.make_async_copy(column_ref.at[mine, :], ocean_ref.at[mine, :], own_ocean_sem)
     own_ocean.start()
 
-    field_in = lax.broadcasted_iota(jnp.int32, (SUB, columns), 0)
-    kept = (field_in >= 2) & (field_in < 5)
-    for level in range(levels):
-        cut = pl.ds(level * SUB, SUB)
-        ended = jnp.where(kept, read_tile(a_ref, cut), read_tile(y_ref, cut))
-        t_ref[cut, :] = ended - read_tile(x_ref, cut)
-
+    for field in (2, 3, 4):
+        for tile in range(levels // SUB):
+            at = tile * SUB * SUB + field
+            write_plane(y_ref, at, SUB, read_plane(a_ref, at, SUB, SUB))
+    mixed_copies = [
+        pltpu.make_async_copy(
+            y_buf.at[block, pl.ds(0, levels)],
+            mixed_ref.at[:, :, pl.ds(block * LANE, LANE)],
+            mixed_sem.at[block],
+        )
+        for block in range(blocks)
+    ]
+    for copy in mixed_copies:
+        copy.start()
+
+    for copy in mixed_copies:
+        copy.wait()
     own_copy.wait()
     own_ocean.wait()
     each(1, all_peers, lambda step: fetch_copy(step).wait_send())
@@ -545,11 +623,14 @@
     each(1, all_peers, lambda step: back_copy(step).wait())
 
 
-def update_kernel(cfg, moments_ref, back_ref, parts_ref, out_ref, ocean_ref, diff_ref):
+def update_kernel(
+    cfg, moments_ref, state_ref, mixed_ref, back_ref, parts_ref, out_ref, tend_ref, ocean_ref, diff_ref
+):
     levels, peers, cap = cfg["levels"], cfg["peers"], cfg["cap"]
     stride, main = cfg["back_stride"], cfg["main"]
     count = len(GRAD_FIELDS) * levels
     block = pl.program_id(0)
+    tend_ref[...] = mixed_ref[...] - state_ref[...]
 
     @pl.when(block == 0)
     def _():
@@ -610,18 +691,13 @@
 SMEM = pl.BlockSpec(memory_space=pltpu.SMEM)
 
 
-def pick_block(array, block):
-    levels, fields, _ = array.shape
-    return pl.BlockSpec((levels, fields, LANE), lambda _: (0, 0, block))
-
-
 def local(state, span_owner, regime, moments, remap_weights, remap_rows, remap_cols):
     peers = lax.axis_size("node") * lax.axis_size("dev")
     levels, fields, columns = state.shape
     slots = moments.shape[2]
     blocks = columns // LANE
     cfg = plan(peers, slots // peers, levels)
-    params = pltpu.CompilerParams(vmem_limit_bytes=48 * 1024 * 1024)
+    params = pltpu.CompilerParams(vmem_limit_bytes=VMEM_BYTES)
 
     floors = lax.axis_size("dev") // 2
     group = 2 * lax.axis_size("node")
@@ -634,28 +710,31 @@
     def copies_of(count):
         return [pltpu.SemaphoreType.DMA((count,))] * 2
 
-    tendencies, back, parts = pl.pallas_call(
+    mixed, back, parts = pl.pallas_call(
         functools.partial(step_kernel, cfg, blocks, slots // LANE),
         out_shape=(
             jax.ShapeDtypeStruct(state.shape, F32),
             jax.ShapeDtypeStruct((peers * cfg["back_stride"], LANE), F32),
             jax.ShapeDtypeStruct((floors * share, LANE), F32),
         ),
-        grid=(1,),
-        in_specs=[pick_block(state, block) for block in range(blocks)]
-        + [pick_block(moments, block) for block in range(slots // LANE)]
-        + [VMEM] * 4
-        + [SMEM] * 2,
-        out_specs=(VMEM, whole, whole),
+        in_specs=[whole, whole, VMEM, VMEM, whole, SMEM, SMEM],
+        out_specs=(whole, whole, whole),
         scratch_shapes=[
+            pltpu.VMEM((blocks, levels, fields, LANE), F32),
+            pltpu.VMEM((slots // LANE, levels, fields, LANE), F32),
+            pltpu.VMEM(remap_weights.shape, F32),
+            pltpu.VMEM((7 * levels, columns), F32),
+            pltpu.VMEM((2 * columns, peers * cfg["fetch_stride"]), BF16),
+            pltpu.VMEM((peers * cfg["main"], columns), BF16),
+            pltpu.VMEM((peers * SUB, columns), BF16),
             rows_of(peers * cfg["fetch_stride"]),
             rows_of(peers * cfg["fetch_stride"]),
             rows_of(peers * cfg["back_stride"]),
             rows_of(group * floors * share),
             rows_of(group * floors * share),
             rows_of(floors * share),
-            rows_of(blocks * (levels + 1) * fields),
-            rows_of(blocks * (levels + 1) * fields),
+            rows_of(blocks * levels * fields),
+            pltpu.VMEM((blocks, levels + 1, fields, LANE), F32),
             rows_of(blocks * levels * fields),
             pltpu.VMEM((levels, columns), F32),
             pltpu.VMEM((levels, columns), F32),
@@ -666,32 +745,41 @@
         + copies_of(peers)
         + copies_of(group)
         + copies_of(floors)
-        + [pltpu.SemaphoreType.DMA, pltpu.SemaphoreType.DMA],
+        + [pltpu.SemaphoreType.DMA, pltpu.SemaphoreType.DMA]
+        + [
+            pltpu.SemaphoreType.DMA((blocks,)),
+            pltpu.SemaphoreType.DMA((slots // LANE,)),
+            pltpu.SemaphoreType.DMA,
+            pltpu.SemaphoreType.DMA((blocks,)),
+        ],
         compiler_params=pltpu.CompilerParams(
-            vmem_limit_bytes=48 * 1024 * 1024, collective_id=0, has_side_effects=True
+            vmem_limit_bytes=VMEM_BYTES, collective_id=0, has_side_effects=True
         ),
     )(
-        *[state] * blocks,
-        *[moments] * (slots // LANE),
-        span_owner,
+        state,
+        moments,
         span_owner.reshape(1, columns),
         regime.reshape(1, columns),
         remap_weights,
         remap_rows,
         remap_cols,
     )
-    moments_out, ocean = pl.pallas_call(
+    steps = slots // LANE
+    by_level = pl.BlockSpec((levels // steps, fields, columns), lambda block: (block, 0, 0))
+    by_slot = pl.BlockSpec((levels, fields, LANE), lambda block: (0, 0, block))
+    moments_out, tendencies, ocean = pl.pallas_call(
         functools.partial(update_kernel, cfg),
         out_shape=(
             jax.ShapeDtypeStruct(moments.shape, F32),
+            jax.ShapeDtypeStruct(state.shape, F32),
             jax.ShapeDtypeStruct((OBLK_DEV * FLUX, LANE), F32),
         ),
-        grid=(slots // LANE,),
-        in_specs=[pl.BlockSpec((levels, fields, LANE), lambda block: (0, 0, block)), VMEM, VMEM],
-        out_specs=(pl.BlockSpec((levels, fields, LANE), lambda block: (0, 0, block)), VMEM),
+        grid=(steps,),
+        in_specs=[by_slot, by_level, by_level, VMEM, VMEM],
+        out_specs=(by_slot, by_level, VMEM),
         scratch_shapes=[pltpu.VMEM((SUB + len(GRAD_FIELDS) * levels, LANE), F32)],
         compiler_params=params,
-    )(moments, back, parts)
+    )(moments, state, mixed, back, parts)
     return (tendencies, moments_out, ocean.reshape(OBLK_DEV, FLUX, LANE))
 
 

time: 48.2 us -> 42.8 us (0.89)
  local copies, waits for them, and re-layouts: 7.57 us -> 0 us
  Pallas kernels: 39.7 us -> 41.9 us
    unnamed x18 -> x0, local copies, waits for them, and re-layouts: 7.57 us -> none
    pallas_call x1, Pallas kernels: 2.21 us -> 4.38 us  [local(): pl.pallas_call(functools.partial(update_kernel, cfg), out_shape=(jax.Shap...]
where the time goes in v3:
time: 42.8 us; the launch traced here: 42.5 us
  Pallas kernels  41.9 us (98%)
  between operations  0.64 us (1%)
    pallas_call x1, Pallas kernels, local(): pl.pallas_call(functools.partial(step_kernel, cfg, blocks, slots // LANE)...  37.5 us
    pallas_call x1, Pallas kernels, local(): pl.pallas_call(functools.partial(update_kernel, cfg), out_shape=(jax.Shap...  4.38 us

profile of v3, /device:TPU:0, one launch (start us, length us, event | category | flops | bytes accessed | tf_op | source)
XLA Modules:
  0.0 42.5 jit_solution(9037991930068421086)
XLA Ops:
  0.6 37.5 %shard_map.94 = (f32[72,8,256]{2,1,0:T(8,128)}, f32[1280,128]{1,0:T(8,128)}, f32[64,128]{1,0:T(8,128)}) custom-call(f32[72,8,256]{2,1,0:T(8,128)} %state_ref.1, f32[72,8,512]{2,1,0:T(8,128)} %moments_ref.1, s32[1,256]{1,0:T(1,128)} %bitcast.3, s32[1,256]{1,0:T(1,128)} %bitcast.4, f32[4,128,128]{2,1,0:T(8,128)} %refs_4_.1, s32[4]{0:T(128)} %refs_5_.1, s32[4]{0:T(128)} %refs_6_.1), custom_call_target="tpu_custom_call" | custom-call | tf_op jit(solution)/shard_map/pallas_call | solution.py:713
  38.2 4.4 %shard_map.95 = (f32[72,8,512]{2,1,0:T(8,128)}, f32[72,8,256]{2,1,0:T(8,128)}, f32[16,128]{1,0:T(8,128)}) custom-call(f32[72,8,512]{2,1,0:T(8,128)} %moments_ref.1, f32[72,8,256]{2,1,0:T(8,128)} %state_ref.1, f32[72,8,256]{2,1,0:T(8,128)} %get-tuple-element.9.mixed_ref, f32[1280,128]{1,0:T(8,128)} %get-tuple-element.10.back_ref, ...), custom_call_target="tpu_custom_call" | custom-call | tf_op jit(solution)/shard_map/pallas_call | solution.py:770

commit v4 on v3

--- a/solution.py
+++ b/solution.py
@@ -255,6 +255,37 @@
     return first, third
 
 
+def update(cfg, m_refs, diff_ref, lanes):
+    levels = cfg["levels"]
+    count = len(GRAD_FIELDS) * levels
+    live = diff_ref[pl.ds(SUB + count - 1, 1), lanes] > 0.5
+    row_in = lax.broadcasted_iota(jnp.int32, (SUB, lanes.size), 0)
+    for tile in range(levels // SUB):
+        grads = []
+        for index in range(len(GRAD_FIELDS)):
+            at = SUB + index * levels + tile * SUB
+            here = diff_ref[pl.ds(at, SUB), lanes]
+            if index == len(GRAD_FIELDS) - 1 and tile == levels // SUB - 1:
+                here = jnp.where(row_in == SUB - 1, 0.0, here)
+            grads.append(here + diff_ref[pl.ds(at - 1, SUB), lanes])
+        grad_u, grad_v, grad_t, grad_q = grads
+        production = [
+            grad_u * grad_u + grad_v * grad_v,
+            grad_t * grad_t,
+            grad_q * grad_q,
+            grad_t * grad_q,
+            grad_u * grad_t,
+            grad_v * grad_t,
+            grad_u * grad_q,
+            grad_u * grad_v,
+        ]
+        for index, value in enumerate(production):
+            at = tile * SUB * SUB + index
+            held = read_plane(m_refs, at, SUB, SUB)
+            new = held + 0.5 * (jnp.tanh(value) - (0.3 + 0.1 * index) * held)
+            write_plane(m_refs, at, SUB, jnp.where(live, new, held))
+
+
 class Links:
     def __init__(self):
         self.nodes, self.devs = lax.axis_size("node"), lax.axis_size("dev")
@@ -293,8 +324,8 @@
         weights_in_ref,
         rows_ref,
         cols_ref,
-        mixed_ref,
-        back_ref,
+        tend_ref,
+        new_ref,
         ocean_ref,
         x_buf,
         m_buf,
@@ -309,6 +340,9 @@
         plane_ref,
         plane_in_ref,
         column_ref,
+        column_in_ref,
+        back_ref,
+        diff_ref,
         a_ref,
         y_buf,
         ratio_ref,
@@ -324,12 +358,9 @@
         plane_recv,
         column_send,
         column_recv,
-        own_sem,
-        own_ocean_sem,
         x_sem,
         m_sem,
         weights_sem,
-        mixed_sem,
     ) = refs
     levels = cfg["levels"]
 
@@ -462,6 +493,62 @@
         return carry
 
     lax.fori_loop(0, TURB_ITERS, again, 0)
+
+    live = lax.broadcasted_iota(jnp.int32, (SUB, columns), 0) == SUB - 1
+    for index, field in enumerate(GRAD_FIELDS):
+        for tile in range(levels // SUB):
+            at = tile * SUB * SUB + field
+            drop = read_plane(y_ref, at, SUB, SUB) - read_plane(y_ref, at + SUB, SUB, SUB)
+            if tile == levels // SUB - 1:
+                ends = 1.0 if index == len(GRAD_FIELDS) - 1 else 0.0
+                drop = jnp.where(live, ends, drop)
+            grad_ref[pl.ds(index * levels + tile * SUB, SUB), :] = drop
+    turn = (((1,), (1,)), ((), ()))
+
+    def place(onehot, values):
+        high, low = split(values)
+        both = lax.dot_general(
+            onehot, jnp.concatenate([high, low], axis=0), turn, preferred_element_type=F32
+        )
+        return both[:, :LANE] + both[:, LANE:]
+
+    size = cfg["back_rest"]
+    tail = grad_ref[pl.ds(2 * LANE, size), :]
+    groups = cap // rows
+    spread = jnp.concatenate(
+        [jnp.where(rank_row // rows == group, tail, 0.0) for group in range(groups)], axis=0
+    )
+    rest = place(put_rest_ref[...], spread)
+    sent = [
+        place(put_ref[...], grad_ref[pl.ds(part * LANE, LANE), :]) for part in range(2)
+    ]
+    halves = main // SUB
+    stride = cfg["back_stride"]
+
+    def offset(half):
+        return 0 if half == 0 else 3 * SUB + (half - 1) * 2 * SUB
+
+    for peer in range(peers):
+        base = peer * stride
+        out_ref[pl.ds(base + 2 * SUB, SUB), :] = rest[peer * SUB : (peer + 1) * SUB]
+        for half in range(halves):
+            for part, value in enumerate(sent):
+                at = peer * main + half * SUB
+                out_ref[pl.ds(base + offset(half) + part * SUB, SUB), :] = value[at : at + SUB]
+
+    def back_copy(half, step):
+        peer = (me + step) % all_peers
+        count = 2 * SUB + (rows if half == 0 else 0)
+        return remote(
+            out_ref.at[pl.ds(peer * stride + offset(half), count), :],
+            back_ref.at[pl.ds(me * stride + offset(half), count), :],
+            back_send.at[half],
+            back_recv.at[half],
+            step,
+            links.coordinates(peer),
+        )
+
+    each(1, all_peers, lambda step: back_copy(0, step).start())
 
     last = pl.ds((levels - 1) * SUB, SUB)
     bottom, bottom_a = read_tile(y_ref, last), read_tile(a_ref, last)
@@ -524,57 +611,25 @@
     mine = pl.ds(pl.multiple_of(here * span, SUB), span)
     plane_in_ref[mine, :] = plane_ref[mine, :]
 
-    live = lax.broadcasted_iota(jnp.int32, (SUB, columns), 0) == SUB - 1
-    for index, field in enumerate(GRAD_FIELDS):
-        for tile in range(levels // SUB):
-            at = tile * SUB * SUB + field
-            drop = read_plane(y_ref, at, SUB, SUB) - read_plane(y_ref, at + SUB, SUB, SUB)
-            if tile == levels // SUB - 1:
-                ends = 1.0 if index == len(GRAD_FIELDS) - 1 else 0.0
-                drop = jnp.where(live, ends, drop)
-            grad_ref[pl.ds(index * levels + tile * SUB, SUB), :] = drop
-    turn = (((1,), (1,)), ((), ()))
-
-    def place(onehot, values):
-        high, low = split(values)
-        both = lax.dot_general(
-            onehot, jnp.concatenate([high, low], axis=0), turn, preferred_element_type=F32
-        )
-        return both[:, :LANE] + both[:, LANE:]
-
-    size = cfg["back_rest"]
-    tail = grad_ref[pl.ds(2 * LANE, size), :]
-    groups = cap // rows
-    spread = jnp.concatenate(
-        [jnp.where(rank_row // rows == group, tail, 0.0) for group in range(groups)], axis=0
-    )
-    sent = [
-        (place(put_ref[...], grad_ref[pl.ds(0, LANE), :]), 0, main),
-        (place(put_ref[...], grad_ref[pl.ds(LANE, LANE), :]), main, main),
-        (place(put_rest_ref[...], spread), 2 * main, SUB),
+    for half in range(1, halves):
+        each(1, all_peers, lambda step: back_copy(half, step).start())
+    own = pl.ds(pl.multiple_of(me * stride, SUB), stride)
+    back_ref[own, :] = out_ref[own, :]
+
+    field_in = lax.broadcasted_iota(jnp.int32, (SUB, columns), 0)
+    kept = (field_in >= 2) & (field_in < 5)
+    for level in range(levels):
+        cut = pl.ds(level * SUB, SUB)
+        ended = jnp.where(kept, read_tile(a_ref, cut), read_tile(y_ref, cut))
+        write_tile(x_ref, cut, ended - read_tile(x_ref, cut))
+    tend_copies = [
+        pltpu.make_async_copy(
+            x_buf.at[block], tend_ref.at[:, :, pl.ds(block * LANE, LANE)], x_sem.at[block]
+        )
+        for block in range(blocks)
     ]
-    for value, at, count in sent:
-        for peer in range(peers):
-            out_ref[pl.ds(peer * cfg["back_stride"] + at, count), :] = value[
-                peer * count : (peer + 1) * count
-            ]
-
-    def back_copy(step):
-        peer = (me + step) % all_peers
-        count = 2 * main + rows
-        return remote(
-            out_ref.at[pl.ds(peer * cfg["back_stride"], count), :],
-            back_ref.at[pl.ds(me * cfg["back_stride"], count), :],
-            back_send,
-            back_recv,
-            step,
-            links.coordinates(peer),
-        )
-
-    each(1, all_peers, lambda step: back_copy(step).start())
-    own = pl.ds(pl.multiple_of(me * cfg["back_stride"], SUB), cfg["back_stride"])
-    own_copy = pltpu.make_async_copy(out_ref.at[own, :], back_ref.at[own, :], own_sem)
-    own_copy.start()
+    for copy in tend_copies:
+        copy.start()
 
     each(1, group, lambda step: plane_copy(step).wait_recv())
     total = plane_in_ref[pl.ds(0, span), :]
@@ -586,7 +641,7 @@
         level = (floor + step) % floors
         return remote(
             column_ref.at[pl.ds(level * share, share), :],
-            ocean_ref.at[pl.ds(floor * share, share), :],
+            column_in_ref.at[pl.ds(floor * share, share), :],
             column_send,
             column_recv,
             step,
@@ -594,97 +649,69 @@
         )
 
     each(1, floors, lambda step: column_copy(step).start())
-    mine = pl.ds(pl.multiple_of(floor * share, SUB), share)
-    own_ocean = pltpu.make_async_copy(column_ref.at[mine, :], ocean_ref.at[mine, :], own_ocean_sem)
-    own_ocean.start()
-
-    for field in (2, 3, 4):
-        for tile in range(levels // SUB):
-            at = tile * SUB * SUB + field
-            write_plane(y_ref, at, SUB, read_plane(a_ref, at, SUB, SUB))
-    mixed_copies = [
-        pltpu.make_async_copy(
-            y_buf.at[block, pl.ds(0, levels)],
-            mixed_ref.at[:, :, pl.ds(block * LANE, LANE)],
-            mixed_sem.at[block],
-        )
-        for block in range(blocks)
-    ]
-    for copy in mixed_copies:
-        copy.start()
-
-    for copy in mixed_copies:
+    moment_blocks = blocks_of(flat_moments, slot_blocks)
+    per_block = LANE // peers
+    per_half = slot_blocks // halves
+    size, count = cfg["back_rest"], len(GRAD_FIELDS) * levels
+    out_copies = []
+    for half in range(halves):
+        each(1, all_peers, lambda step: back_copy(half, step).wait_recv())
+        if half == 0:
+            turned = jnp.concatenate(
+                [back_ref[pl.ds(2 * SUB + row, peers, stride=stride), :] for row in range(rows)],
+                axis=0,
+            ).T
+        mine = range(half * per_half, (half + 1) * per_half)
+        for block in mine:
+            lanes = pl.ds(block * LANE, LANE)
+            diff_ref[pl.ds(0, SUB), lanes] = jnp.zeros((SUB, LANE), F32)
+            for part in range(2):
+                start = offset(half) + part * SUB + block * per_block - half * SUB
+                picked = [
+                    back_ref[pl.ds(start + slot, peers, stride=stride), :]
+                    for slot in range(per_block)
+                ]
+                at = SUB + part * LANE
+                diff_ref[pl.ds(at, LANE), lanes] = jnp.concatenate(picked, axis=0).T
+            diff_ref[pl.ds(SUB + 2 * LANE, size), lanes] = turned[block * size : (block + 1) * size]
+        lanes = pl.ds(half * per_half * LANE, per_half * LANE)
+        update(cfg, moment_blocks[mine.start : mine.stop], diff_ref, lanes)
+        for block in mine:
+            copy = pltpu.make_async_copy(
+                m_buf.at[block], new_ref.at[:, :, pl.ds(block * LANE, LANE)], m_sem.at[block]
+            )
+            copy.start()
+            out_copies.append(copy)
+
+    each(1, floors, lambda step: column_copy(step).wait_recv())
+    total = column_ref[pl.ds(pl.multiple_of(floor * share, SUB), share), :]
+    for step in range(1, floors):
+        level = (floor + step) % floors
+        total = total + column_in_ref[pl.ds(pl.multiple_of(level * share, SUB), share), :]
+    ocean_ref[...] = total
+
+    for copy in tend_copies + out_copies:
         copy.wait()
-    own_copy.wait()
-    own_ocean.wait()
     each(1, all_peers, lambda step: fetch_copy(step).wait_send())
     each(1, group, lambda step: plane_copy(step).wait_send())
-    each(1, floors, lambda step: column_copy(step).wait())
-    each(1, all_peers, lambda step: back_copy(step).wait())
-
-
-def update_kernel(
-    cfg, moments_ref, state_ref, mixed_ref, back_ref, parts_ref, out_ref, tend_ref, ocean_ref, diff_ref
-):
-    levels, peers, cap = cfg["levels"], cfg["peers"], cfg["cap"]
-    stride, main = cfg["back_stride"], cfg["main"]
-    count = len(GRAD_FIELDS) * levels
-    block = pl.program_id(0)
-    tend_ref[...] = mixed_ref[...] - state_ref[...]
-
-    @pl.when(block == 0)
-    def _():
-        share = OBLK_DEV * FLUX
-        total = parts_ref[pl.ds(0, share), :]
-        for floor in range(1, parts_ref.shape[0] // share):
-            total = total + parts_ref[pl.ds(floor * share, share), :]
-        ocean_ref[...] = total
-
-    width = LANE // peers
-    for part in range(2):
-        rows = [
-            back_ref[pl.ds(part * main + block * width + slot, peers, stride=stride), :]
-            for slot in range(width)
-        ]
-        diff_ref[pl.ds(SUB + part * LANE, LANE), :] = jnp.concatenate(rows, axis=0).T
-    rows, size = cfg["back_rows"], cfg["back_rest"]
-    turned = jnp.concatenate(
-        [back_ref[pl.ds(2 * main + row, peers, stride=stride), :] for row in range(rows)], axis=0
-    ).T
-    tail = jnp.zeros((size, LANE), F32)
-    for group in range(cap // rows):
-        tail = jnp.where(block == group, turned[group * size : (group + 1) * size], tail)
-    diff_ref[pl.ds(SUB + 2 * LANE, size), :] = tail
-    diff_ref[pl.ds(0, SUB), :] = jnp.zeros((SUB, LANE), F32)
-
-    m_ref = [moments_ref.reshape(levels * SUB, LANE)]
-    o_ref = [out_ref.reshape(levels * SUB, LANE)]
-    live = diff_ref[pl.ds(SUB + count - 1, 1), :] > 0.5
-    row_in = lax.broadcasted_iota(jnp.int32, (SUB, LANE), 0)
-    for tile in range(levels // SUB):
-        grads = []
-        for index in range(len(GRAD_FIELDS)):
-            at = SUB + index * levels + tile * SUB
-            here = diff_ref[pl.ds(at, SUB), :]
-            if index == len(GRAD_FIELDS) - 1 and tile == levels // SUB - 1:
-                here = jnp.where(row_in == SUB - 1, 0.0, here)
-            grads.append(here + diff_ref[pl.ds(at - 1, SUB), :])
-        grad_u, grad_v, grad_t, grad_q = grads
-        production = [
-            grad_u * grad_u + grad_v * grad_v,
-            grad_t * grad_t,
-            grad_q * grad_q,
-            grad_t * grad_q,
-            grad_u * grad_t,
-            grad_v * grad_t,
-            grad_u * grad_q,
-            grad_u * grad_v,
-        ]
-        for index, value in enumerate(production):
-            at = tile * SUB * SUB + index
-            held = read_plane(m_ref, at, SUB, SUB)
-            new = held + 0.5 * (jnp.tanh(value) - (0.3 + 0.1 * index) * held)
-            write_plane(o_ref, at, SUB, jnp.where(live, new, held))
+    each(1, floors, lambda step: column_copy(step).wait_send())
+    for half in range(halves):
+        each(1, all_peers, lambda step: back_copy(half, step).wait_send())
+
+
+def copy_kernel(pieces, *refs):
+    count = len(refs) // 2
+    sources, targets, sems = refs[:count], refs[count:-1], refs[-1]
+    copies = []
+    for source, target in zip(sources, targets):
+        size = max(1, source.shape[0] // pieces)
+        for start in range(0, source.shape[0], size):
+            cut = pl.ds(start, min(size, source.shape[0] - start))
+            copies.append(pltpu.make_async_copy(source.at[cut], target.at[cut], sems.at[len(copies)]))
+    for copy in copies:
+        copy.start()
+    for copy in copies:
+        copy.wait()
 
 
 VMEM = pl.BlockSpec(memory_space=pltpu.VMEM)
@@ -710,15 +737,15 @@
     def copies_of(count):
         return [pltpu.SemaphoreType.DMA((count,))] * 2
 
-    mixed, back, parts = pl.pallas_call(
+    results = pl.pallas_call(
         functools.partial(step_kernel, cfg, blocks, slots // LANE),
         out_shape=(
             jax.ShapeDtypeStruct(state.shape, F32),
-            jax.ShapeDtypeStruct((peers * cfg["back_stride"], LANE), F32),
-            jax.ShapeDtypeStruct((floors * share, LANE), F32),
+            jax.ShapeDtypeStruct(moments.shape, F32),
+            jax.ShapeDtypeStruct((share, LANE), F32),
         ),
         in_specs=[whole, whole, VMEM, VMEM, whole, SMEM, SMEM],
-        out_specs=(whole, whole, whole),
+        out_specs=(whole, whole, VMEM),
         scratch_shapes=[
             pltpu.VMEM((blocks, levels, fields, LANE), F32),
             pltpu.VMEM((slots // LANE, levels, fields, LANE), F32),
@@ -733,6 +760,9 @@
             rows_of(group * floors * share),
             rows_of(group * floors * share),
             rows_of(floors * share),
+            rows_of(floors * share),
+            rows_of(peers * cfg["back_stride"]),
+            pltpu.VMEM((SUB + len(GRAD_FIELDS) * levels, slots), F32),
             rows_of(blocks * levels * fields),
             pltpu.VMEM((blocks, levels + 1, fields, LANE), F32),
             rows_of(blocks * levels * fields),
@@ -742,15 +772,13 @@
             pltpu.VMEM((len(GRAD_FIELDS) * levels, columns), F32),
         ]
         + copies_of(peers)
-        + copies_of(peers)
+        + [pltpu.SemaphoreType.DMA((cfg["main"] // SUB, peers))] * 2
         + copies_of(group)
         + copies_of(floors)
-        + [pltpu.SemaphoreType.DMA, pltpu.SemaphoreType.DMA]
         + [
             pltpu.SemaphoreType.DMA((blocks,)),
             pltpu.SemaphoreType.DMA((slots // LANE,)),
             pltpu.SemaphoreType.DMA,
-            pltpu.SemaphoreType.DMA((blocks,)),
         ],
         compiler_params=pltpu.CompilerParams(
             vmem_limit_bytes=VMEM_BYTES, collective_id=0, has_side_effects=True
@@ -764,22 +792,15 @@
         remap_rows,
         remap_cols,
     )
-    steps = slots // LANE
-    by_level = pl.BlockSpec((levels // steps, fields, columns), lambda block: (block, 0, 0))
-    by_slot = pl.BlockSpec((levels, fields, LANE), lambda block: (0, 0, block))
-    moments_out, tendencies, ocean = pl.pallas_call(
-        functools.partial(update_kernel, cfg),
-        out_shape=(
-            jax.ShapeDtypeStruct(moments.shape, F32),
-            jax.ShapeDtypeStruct(state.shape, F32),
-            jax.ShapeDtypeStruct((OBLK_DEV * FLUX, LANE), F32),
-        ),
-        grid=(steps,),
-        in_specs=[by_slot, by_level, by_level, VMEM, VMEM],
-        out_specs=(by_slot, by_level, VMEM),
-        scratch_shapes=[pltpu.VMEM((SUB + len(GRAD_FIELDS) * levels, LANE), F32)],
+    pieces = 8
+    tendencies, moments_out, ocean = pl.pallas_call(
+        functools.partial(copy_kernel, pieces),
+        out_shape=tuple(jax.ShapeDtypeStruct(result.shape, F32) for result in results),
+        in_specs=[whole] * 3,
+        out_specs=(whole,) * 3,
+        scratch_shapes=[pltpu.SemaphoreType.DMA((3 * pieces + 3,))],
         compiler_params=params,
-    )(moments, state, mixed, back, parts)
+    )(*results)
     return (tendencies, moments_out, ocean.reshape(OBLK_DEV, FLUX, LANE))
 
 

time: 42.8 us -> 95.7 us (2.24)
  Pallas kernels: 41.9 us -> 94.9 us
    pallas_call x1, Pallas kernels: 4.38 us -> 55.2 us  [local(): pl.pallas_call(functools.partial(copy_kernel, pieces), out_shape=tuple((j...]
    pallas_call x1, Pallas kernels: 37.5 us -> 39.7 us  [local(): pl.pallas_call(functools.partial(step_kernel, cfg, blocks, slots // LANE)...]
where the time goes in v4:
time: 95.7 us; the launch traced here: 95.6 us
  Pallas kernels  94.9 us (99%)
    pallas_call x1, Pallas kernels, local(): pl.pallas_call(functools.partial(copy_kernel, pieces), out_shape=tuple((j...  55.2 us
    pallas_call x1, Pallas kernels, local(): pl.pallas_call(functools.partial(step_kernel, cfg, blocks, slots // LANE)...  39.7 us

profile of v4, /device:TPU:0, one launch (start us, length us, event | category | flops | bytes accessed | tf_op | source)
XLA Modules:
  0.0 95.6 jit_solution(9610492235639867910)
XLA Ops:
  0.6 39.7 %shard_map.94 = (f32[72,8,256]{2,1,0:T(8,128)}, f32[72,8,512]{2,1,0:T(8,128)}, f32[16,128]{1,0:T(8,128)}) custom-call(f32[72,8,256]{2,1,0:T(8,128)} %refs_0_.1, f32[72,8,512]{2,1,0:T(8,128)} %refs_1_.1, s32[1,256]{1,0:T(1,128)} %bitcast.3, s32[1,256]{1,0:T(1,128)} %bitcast.4, f32[4,128,128]{2,1,0:T(8,128)} %refs_4_.1, s32[4]{0:T(128)} %refs_5_.1, s32[4]{0:T(128)} %refs_6_.1), custom_call_target="tpu_custom_call" | custom-call | tf_op jit(solution)/shard_map/pallas_call | solution.py:740
  40.4 55.2 %shard_map.95 = (f32[72,8,256]{2,1,0:T(8,128)}, f32[72,8,512]{2,1,0:T(8,128)}, f32[16,128]{1,0:T(8,128)}) custom-call(f32[72,8,256]{2,1,0:T(8,128)} %get-tuple-element.9.refs_0_, f32[72,8,512]{2,1,0:T(8,128)} %get-tuple-element.10.refs_1_, f32[16,128]{1,0:T(8,128)} %get-tuple-element.11.refs_2_), custom_call_target="tpu_custom_call" | custom-call | tf_op jit(solution)/shard_map/pallas_call | solution.py:796

commit v5 on v4

--- a/solution.py
+++ b/solution.py
@@ -13,7 +13,7 @@
 LANE = 128
 SUB = 8
 FLUX = 4
-VMEM_BYTES = 60 * 1024 * 1024
+VMEM_BYTES = 58 * 1024 * 1024
 GRAD_FIELDS = (5, 6, 0, 1)
 F32 = jnp.float32
 BF16 = jnp.bfloat16
@@ -324,11 +324,9 @@
         weights_in_ref,
         rows_ref,
         cols_ref,
-        tend_ref,
-        new_ref,
-        ocean_ref,
         x_buf,
         m_buf,
+        ocean_ref,
         weights_ref,
         early_ref,
         pick_ref,
@@ -622,15 +620,6 @@
         cut = pl.ds(level * SUB, SUB)
         ended = jnp.where(kept, read_tile(a_ref, cut), read_tile(y_ref, cut))
         write_tile(x_ref, cut, ended - read_tile(x_ref, cut))
-    tend_copies = [
-        pltpu.make_async_copy(
-            x_buf.at[block], tend_ref.at[:, :, pl.ds(block * LANE, LANE)], x_sem.at[block]
-        )
-        for block in range(blocks)
-    ]
-    for copy in tend_copies:
-        copy.start()
-
     each(1, group, lambda step: plane_copy(step).wait_recv())
     total = plane_in_ref[pl.ds(0, span), :]
     for member in range(1, group):
@@ -653,7 +642,6 @@
     per_block = LANE // peers
     per_half = slot_blocks // halves
     size, count = cfg["back_rest"], len(GRAD_FIELDS) * levels
-    out_copies = []
     for half in range(halves):
         each(1, all_peers, lambda step: back_copy(half, step).wait_recv())
         if half == 0:
@@ -676,12 +664,6 @@
             diff_ref[pl.ds(SUB + 2 * LANE, size), lanes] = turned[block * size : (block + 1) * size]
         lanes = pl.ds(half * per_half * LANE, per_half * LANE)
         update(cfg, moment_blocks[mine.start : mine.stop], diff_ref, lanes)
-        for block in mine:
-            copy = pltpu.make_async_copy(
-                m_buf.at[block], new_ref.at[:, :, pl.ds(block * LANE, LANE)], m_sem.at[block]
-            )
-            copy.start()
-            out_copies.append(copy)
 
     each(1, floors, lambda step: column_copy(step).wait_recv())
     total = column_ref[pl.ds(pl.multiple_of(floor * share, SUB), share), :]
@@ -690,8 +672,6 @@
         total = total + column_in_ref[pl.ds(pl.multiple_of(level * share, SUB), share), :]
     ocean_ref[...] = total
 
-    for copy in tend_copies + out_copies:
-        copy.wait()
     each(1, all_peers, lambda step: fetch_copy(step).wait_send())
     each(1, group, lambda step: plane_copy(step).wait_send())
     each(1, floors, lambda step: column_copy(step).wait_send())
@@ -699,15 +679,12 @@
         each(1, all_peers, lambda step: back_copy(half, step).wait_send())
 
 
-def copy_kernel(pieces, *refs):
-    count = len(refs) // 2
-    sources, targets, sems = refs[:count], refs[count:-1], refs[-1]
-    copies = []
-    for source, target in zip(sources, targets):
-        size = max(1, source.shape[0] // pieces)
-        for start in range(0, source.shape[0], size):
-            cut = pl.ds(start, min(size, source.shape[0] - start))
-            copies.append(pltpu.make_async_copy(source.at[cut], target.at[cut], sems.at[len(copies)]))
+def write_kernel(tend_in_ref, moments_in_ref, ocean_in_ref, tend_ref, moments_ref, ocean_ref, sems):
+    copies = [pltpu.make_async_copy(ocean_in_ref, ocean_ref, sems.at[0])]
+    for source, target in ((moments_in_ref, moments_ref), (tend_in_ref, tend_ref)):
+        for block in range(source.shape[0]):
+            place = target.at[:, :, pl.ds(block * LANE, LANE)]
+            copies.append(pltpu.make_async_copy(source.at[block], place, sems.at[len(copies)]))
     for copy in copies:
         copy.start()
     for copy in copies:
@@ -724,7 +701,7 @@
     slots = moments.shape[2]
     blocks = columns // LANE
     cfg = plan(peers, slots // peers, levels)
-    params = pltpu.CompilerParams(vmem_limit_bytes=VMEM_BYTES)
+    params = pltpu.CompilerParams(vmem_limit_bytes=8 * 1024 * 1024)
 
     floors = lax.axis_size("dev") // 2
     group = 2 * lax.axis_size("node")
@@ -740,15 +717,13 @@
     results = pl.pallas_call(
         functools.partial(step_kernel, cfg, blocks, slots // LANE),
         out_shape=(
-            jax.ShapeDtypeStruct(state.shape, F32),
-            jax.ShapeDtypeStruct(moments.shape, F32),
-            jax.ShapeDtypeStruct((share, LANE), F32),
+            pltpu.VMEM((blocks, levels, fields, LANE), F32),
+            pltpu.VMEM((slots // LANE, levels, fields, LANE), F32),
+            pltpu.VMEM((share, LANE), F32),
         ),
         in_specs=[whole, whole, VMEM, VMEM, whole, SMEM, SMEM],
-        out_specs=(whole, whole, VMEM),
+        out_specs=(VMEM, VMEM, VMEM),
         scratch_shapes=[
-            pltpu.VMEM((blocks, levels, fields, LANE), F32),
-            pltpu.VMEM((slots // LANE, levels, fields, LANE), F32),
             pltpu.VMEM(remap_weights.shape, F32),
             pltpu.VMEM((7 * levels, columns), F32),
             pltpu.VMEM((2 * columns, peers * cfg["fetch_stride"]), BF16),
@@ -792,13 +767,16 @@
         remap_rows,
         remap_cols,
     )
-    pieces = 8
     tendencies, moments_out, ocean = pl.pallas_call(
-        functools.partial(copy_kernel, pieces),
-        out_shape=tuple(jax.ShapeDtypeStruct(result.shape, F32) for result in results),
+        write_kernel,
+        out_shape=(
+            jax.ShapeDtypeStruct(state.shape, F32),
+            jax.ShapeDtypeStruct(moments.shape, F32),
+            jax.ShapeDtypeStruct((share, LANE), F32),
+        ),
         in_specs=[whole] * 3,
         out_specs=(whole,) * 3,
-        scratch_shapes=[pltpu.SemaphoreType.DMA((3 * pieces + 3,))],
+        scratch_shapes=[pltpu.SemaphoreType.DMA((1 + blocks + slots // LANE,))],
         compiler_params=params,
     )(*results)
     return (tendencies, moments_out, ocean.reshape(OBLK_DEV, FLUX, LANE))

time: 95.7 us -> 40.4 us (0.42)
  Pallas kernels: 94.9 us -> 39.6 us
    pallas_call x1, Pallas kernels: 55.2 us -> 1.27 us  [local(): pl.pallas_call(write_kernel, out_shape=(jax.ShapeDtypeStruct(state.shape,...]
    pallas_call x1, Pallas kernels: 39.7 us -> 38.3 us  [local(): pl.pallas_call(functools.partial(step_kernel, cfg, blocks, slots // LANE)...]
where the time goes in v5:
time: 40.4 us; the launch traced here: 40.2 us
  Pallas kernels  39.6 us (98%)
  between operations  0.64 us (2%)
    pallas_call x1, Pallas kernels, local(): pl.pallas_call(functools.partial(step_kernel, cfg, blocks, slots // LANE)...  38.3 us
    pallas_call x1, Pallas kernels, local(): pl.pallas_call(write_kernel, out_shape=(jax.ShapeDtypeStruct(state.shape,...  1.27 us

profile of v5, /device:TPU:0, one launch (start us, length us, event | category | flops | bytes accessed | tf_op | source)
XLA Modules:
  0.0 40.2 jit_solution(14541580593877253940)
XLA Ops:
  0.6 38.3 %shard_map.94 = (f32[2,72,8,128]{3,2,1,0:T(8,128)S(1)}, f32[4,72,8,128]{3,2,1,0:T(8,128)S(1)}, f32[16,128]{1,0:T(8,128)S(1)}) custom-call(f32[72,8,256]{2,1,0:T(8,128)} %refs_0_.1, f32[72,8,512]{2,1,0:T(8,128)} %refs_1_.1, s32[1,256]{1,0:T(1,128)} %bitcast.3, s32[1,256]{1,0:T(1,128)} %bitcast.4, f32[4,128,128]{2,1,0:T(8,128)} %refs_4_.1, s32[4]{0:T(128)} %refs_5_.1, ...), custom_call_target="tpu_custom_call" | custom-call | tf_op jit(solution)/shard_map/pallas_call | solution.py:717
  38.9 1.3 %shard_map.95 = (f32[72,8,256]{2,1,0:T(8,128)}, f32[72,8,512]{2,1,0:T(8,128)}, f32[16,128]{1,0:T(8,128)}) custom-call(f32[2,72,8,128]{3,2,1,0:T(8,128)S(1)} %get-tuple-element.9.tend_in_ref, f32[4,72,8,128]{3,2,1,0:T(8,128)S(1)} %get-tuple-element.10.moments_in_ref, f32[16,128]{1,0:T(8,128)S(1)} %get-tuple-element.11.ocean_in_ref), custom_call_target="tpu_custom_call" | custom-call | tf_op jit(solution)/shard_map/pallas_call | solution.py:770
